TPU v7x, 512 devices: a whole 4x8x8 slice. The times are simulated.
512 devices in a mesh: lon: 64 (over z, y_hi, core), lat: 8 (over x, y_lo).
Axes of the slice: x: 4, y: 8 (y_hi: 4, y_lo: 2; y = y_hi * 2 + y_lo), z: 8, core: 2. Of those that a mesh axis runs over, the one named last changes fastest.
Arguments:
- patches: bfloat16 [64, 512, 276], P('lat', 'lon')
- query_weight: bfloat16 [1024, 512], P(None, 'lon')
- key_weight: bfloat16 [1024, 512], P(None, 'lon')
- value_weight: bfloat16 [1024, 512], P(None, 'lon'), may hold values from -0.1875 to 0.1875
- out_weight: bfloat16 [512, 1024], P(None, 'lon'), may hold values from -0.25 to 0.25
- embed_weight: bfloat16 [276, 1024], P(None, 'lon'), may hold values from -0.0390625 to 0.0390625
- cotangent: bfloat16 [64, 512, 1024], P('lat', 'lon'), may hold values from -6 to 6
Outputs:
- block_out: bfloat16 [64, 512, 1024], P('lat', 'lon')
- patch_grad: bfloat16 [64, 512, 276], P('lat', 'lon')
All inputs are finite; a program needn't handle non-finite values.
Results may differ from a plain program's by a relative error of at most 0.025.
The roundings to bfloat16 on the way count: a program that leaves them out, or rounds other values in their place, can miss the bound.
Values may be sent and summed in bfloat16 or wider, within the bound.
A program may use at most 64 MiB of HBM per device.

v0:
```python
import math

import jax
import jax.numpy as jnp
from jax import lax
from jax.sharding import PartitionSpec as P

HEADS = 8
RAD = 6
PAD = 6


def with_halo(block, sides, width, periodic):
    for axis, dim in sides:
        count = lax.axis_size(axis)
        forward = [(i, i + 1) for i in range(count - 1)]
        if periodic:
            forward.append((count - 1, 0))
        backward = [(target, source) for source, target in forward]
        low = lax.ppermute(
            lax.slice_in_dim(block, block.shape[dim] - width, None, axis=dim), axis, forward
        )
        high = lax.ppermute(lax.slice_in_dim(block, 0, width, axis=dim), axis, backward)
        block = jnp.concatenate([low, block, high], axis=dim)
    return block


def layer_norm(embedded):
    centre = jnp.mean(embedded, axis=-1, keepdims=True)
    centred = embedded - centre
    inv_std = lax.rsqrt(jnp.mean(centred * centred, axis=-1, keepdims=True) + 1e-05)
    return (centred * inv_std, inv_std)


def head_dot(left, right):
    return jnp.einsum("rche,rche->rch", left, right, preferred_element_type=jnp.float32)


def head_scale(weight, grid):
    return jnp.einsum("rch,rche->rche", weight, grid, preferred_element_type=jnp.float32)


def window_pass(queries, grad_attn, key_ext, value_ext, key_ok):
    row_count, col_count, channels = queries.shape
    head_size = channels // HEADS
    reach = 2 * RAD + 1
    score_scale = 1.0 / math.sqrt(head_size)
    q_heads = queries.reshape(row_count, col_count, HEADS, head_size)
    g_heads = grad_attn.reshape(row_count, col_count, HEADS, head_size)

    def take_piece(slab, offset):
        return slab[:, offset : offset + col_count].reshape(row_count, col_count, HEADS, head_size)

    def first(carried, shift_row):
        key_slab = lax.dynamic_slice_in_dim(key_ext, shift_row, row_count, 0)
        value_slab = lax.dynamic_slice_in_dim(value_ext, shift_row, row_count, 0)
        raw = [head_dot(q_heads, take_piece(key_slab, offset)) for offset in range(reach)]
        slope = [head_dot(g_heads, take_piece(value_slab, offset)) for offset in range(reach)]
        return (carried, (jnp.stack(raw, -1), jnp.stack(slope, -1)))

    shifts = jnp.arange(reach, dtype=jnp.int32)
    unused, (scores, dprob) = lax.scan(first, jnp.int32(0), shifts)
    row_mask = jnp.stack([key_ok[shift : shift + row_count] for shift in range(reach)], 0)
    allowed = row_mask[:, :, None, None, None] > 0.5
    scores = jnp.where(allowed, scores * score_scale, -jnp.inf)
    row_top = jnp.max(scores, axis=(0, 4), keepdims=True)
    exp_terms = jnp.exp(scores - row_top)
    row_total = jnp.sum(exp_terms, axis=(0, 4), keepdims=True)
    prob = exp_terms / row_total
    log_total = (row_top + jnp.log(row_total))[0, :, :, :, 0]
    row_delta = jnp.sum(prob * dprob, axis=(0, 4))
    dscore = (prob * (dprob - row_delta[None, :, :, :, None])).astype(jnp.bfloat16)
    prob_b = prob.astype(jnp.bfloat16)
    head_zero = jnp.zeros((row_count, col_count, HEADS, head_size), jnp.float32)
    ext_zero = jnp.zeros(key_ext.shape, jnp.float32)

    def second(carried, shift_row):
        attended, grad_q, grad_k, grad_v = carried
        key_slab = lax.dynamic_slice_in_dim(key_ext, shift_row, row_count, 0)
        value_slab = lax.dynamic_slice_in_dim(value_ext, shift_row, row_count, 0)
        p_row = lax.dynamic_index_in_dim(prob_b, shift_row, 0, keepdims=False)
        s_row = lax.dynamic_index_in_dim(dscore, shift_row, 0, keepdims=False)
        slab_k = jnp.zeros((row_count, col_count + 2 * RAD, channels), jnp.float32)
        slab_v = jnp.zeros((row_count, col_count + 2 * RAD, channels), jnp.float32)
        for offset in range(reach):
            attended = attended + head_scale(p_row[..., offset], take_piece(value_slab, offset))
            grad_q = grad_q + head_scale(s_row[..., offset], take_piece(key_slab, offset))
            spread = ((0, 0), (offset, reach - 1 - offset), (0, 0))
            slab_k = slab_k + jnp.pad(
                head_scale(s_row[..., offset], q_heads).reshape(row_count, col_count, channels),
                spread,
            )
            slab_v = slab_v + jnp.pad(
                head_scale(p_row[..., offset], g_heads).reshape(row_count, col_count, channels),
                spread,
            )
        grad_k = lax.dynamic_update_slice_in_dim(
            grad_k, lax.dynamic_slice_in_dim(grad_k, shift_row, row_count, 0) + slab_k, shift_row, 0
        )
        grad_v = lax.dynamic_update_slice_in_dim(
            grad_v, lax.dynamic_slice_in_dim(grad_v, shift_row, row_count, 0) + slab_v, shift_row, 0
        )
        return ((attended, grad_q, grad_k, grad_v), None)

    (attended, grad_q, grad_k, grad_v), unused = lax.scan(
        second, (head_zero, head_zero, ext_zero, ext_zero), shifts
    )
    attended = attended.reshape(row_count, col_count, channels).astype(jnp.bfloat16)
    grad_q = (grad_q * score_scale).reshape(row_count, col_count, channels).astype(jnp.bfloat16)
    return (attended, grad_q, grad_k * score_scale, grad_v, log_total, row_delta)


def fold_back(grad_k, grad_v, row_count, col_count):
    stacked = jnp.stack((grad_k, grad_v), 0)
    rims = jnp.concatenate((stacked[:, :RAD], stacked[:, row_count + RAD :]), 1)
    arrived = with_halo(rims, (("lat", 1),), RAD, False)
    middle = stacked[:, RAD : row_count + RAD]
    middle = middle.at[:, :RAD].add(arrived[:, :RAD])
    middle = middle.at[:, row_count - RAD :].add(arrived[:, 3 * RAD :])
    sides = jnp.concatenate((middle[:, :, :RAD], middle[:, :, col_count + RAD :]), 2)
    landed = with_halo(sides, (("lon", 2),), RAD, True)
    owned = middle[:, :, RAD : col_count + RAD]
    owned = owned.at[:, :, :RAD].add(landed[:, :, :RAD])
    owned = owned.at[:, :, col_count - RAD :].add(landed[:, :, 3 * RAD :])
    return (owned[0].astype(jnp.bfloat16), owned[1].astype(jnp.bfloat16))


def body(patches, query_weight, key_weight, value_weight, out_weight, embed_weight, cotangent):
    row_count, col_count, patch_width = patches.shape
    w_query, w_key, w_value, w_out, w_embed = (
        lax.all_gather(query_weight, "lon", axis=1, tiled=True),
        lax.all_gather(key_weight, "lon", axis=1, tiled=True),
        lax.all_gather(value_weight, "lon", axis=1, tiled=True),
        lax.all_gather(out_weight, "lon", axis=1, tiled=True),
        lax.all_gather(embed_weight, "lon", axis=1, tiled=True),
    )
    width = w_embed.shape[1]
    channels = w_query.shape[1]
    lats = row_count * lax.axis_size("lat") - PAD
    first_row = lax.axis_index("lat") * row_count
    own_ids = first_row + jnp.arange(row_count, dtype=jnp.int32)
    row_valid = (own_ids < lats).astype(jnp.float32)
    valid_cells = jnp.repeat(row_valid, col_count)[:, None]
    ext_ids = first_row + jnp.arange(row_count + 2 * RAD, dtype=jnp.int32) - RAD
    ext_ok = ((ext_ids >= 0) & (ext_ids < lats)).astype(jnp.float32)
    embedded = jnp.dot(
        patches.reshape(row_count * col_count, patch_width),
        w_embed,
        preferred_element_type=jnp.float32,
    )
    normal, inv_std = layer_norm(embedded)
    normed = normal.astype(jnp.bfloat16)

    def project(weight):
        return (
            jnp.dot(normed, weight, preferred_element_type=jnp.float32)
            .astype(jnp.bfloat16)
            .reshape(row_count, col_count, channels)
        )

    queries = project(w_query)
    keys_grid = project(w_key)
    values_grid = project(w_value)
    paired = with_halo(jnp.stack((keys_grid, values_grid), 0), (("lon", 2), ("lat", 1)), RAD, True)
    masked = cotangent.reshape(row_count * col_count, width).astype(jnp.float32) * valid_cells
    grad_attn = jnp.dot(masked.astype(jnp.bfloat16), w_out.T, preferred_element_type=jnp.float32)
    grad_attn = grad_attn.astype(jnp.bfloat16).reshape(row_count, col_count, channels)
    attended, grad_query, key_sum, value_sum, log_total, row_delta = window_pass(
        queries, grad_attn, paired[0], paired[1], ext_ok
    )
    grad_key, grad_value = fold_back(key_sum, value_sum, row_count, col_count)
    attended = attended.reshape(row_count * col_count, channels)
    mixed = embedded + jnp.dot(attended, w_out, preferred_element_type=jnp.float32)
    block_out = (mixed * valid_cells).astype(jnp.bfloat16).reshape(row_count, col_count, width)
    grad_normed = jnp.dot(
        grad_query.reshape(-1, channels), w_query.T, preferred_element_type=jnp.float32
    )
    grad_normed = grad_normed + jnp.dot(
        grad_key.reshape(-1, channels), w_key.T, preferred_element_type=jnp.float32
    )
    grad_normed = grad_normed + jnp.dot(
        grad_value.reshape(-1, channels), w_value.T, preferred_element_type=jnp.float32
    )
    centre_grad = jnp.mean(grad_normed, axis=-1, keepdims=True)
    along = jnp.mean(grad_normed * normal, axis=-1, keepdims=True)
    grad_embed = (masked + inv_std * (grad_normed - centre_grad - normal * along)).astype(
        jnp.bfloat16
    )
    patch_grad = jnp.dot(grad_embed, w_embed.T, preferred_element_type=jnp.float32)
    patch_grad = patch_grad.astype(jnp.bfloat16).reshape(row_count, col_count, patch_width)
    return (block_out, patch_grad)


def solution(mesh):
    in_specs = (
        P("lat", "lon", None),
        P(None, "lon"),
        P(None, "lon"),
        P(None, "lon"),
        P(None, "lon"),
        P(None, "lon"),
        P("lat", "lon", None),
    )
    out_specs = (P("lat", "lon", None), P("lat", "lon", None))
    return jax.shard_map(body, mesh=mesh, in_specs=in_specs, out_specs=out_specs, check_vma=False)
```

profile of v0, /device:TPU:3, one launch (start us, length us, event | category | flops | bytes accessed | tf_op | source)
XLA Modules:
  0.0 1683.8 jit_solution(8240100868773661833)
XLA Ops:
  10.1 92.5 %all_gather.15 = bf16[276,1024]{0,1:T(8,128)(2,1)S(1)} all-gather(bf16[276,16]{0,1:T(8,128)(2,1)} %param.24), channel_id=1, replica_groups=mesh['lon'=64,'lat'=8] {'lon'}, dimensions={1}, use_global_device_ids=true | all-gather | bytes 574080 | tf_op jit(solution)/shard_map/all_gather | solution.py:135
  105.3 77.0 %all-gather.7.cloned.1.call-done = bf16[1024,512]{0,1:T(8,128)(2,1)} async-done(((bf16[1024,8]{0,1:T(8,128)(2,1)}), bf16[1024,512]{0,1:T(8,128)(2,1)}) %all-gather.7.cloned.1.call-update) | async-done | bytes 1048592 | tf_op jit(solution)/shard_map/all_gather | solution.py:133
  184.0 4.0 collective-permute-start
  190.0 75.0 %all-gather.9.cloned.1.call-done = bf16[1024,512]{0,1:T(8,128)(2,1)} async-done(((bf16[1024,8]{0,1:T(8,128)(2,1)}), bf16[1024,512]{0,1:T(8,128)(2,1)}) %all-gather.9.cloned.1.call-update) | async-done | bytes 1048592 | tf_op jit(solution)/shard_map/all_gather | solution.py:131
  269.3 4.1 collective-permute-start.3
  273.4 74.2 %all-gather.11.cloned.1.call-done = bf16[512,1024]{0,1:T(8,128)(2,1)} async-done(((bf16[512,16]{0,1:T(8,128)(2,1)}), bf16[512,1024]{0,1:T(8,128)(2,1)}) %all-gather.11.cloned.1.call-update) | async-done | bytes 1048592 | tf_op jit(solution)/shard_map/all_gather | solution.py:134
  349.6 130.0 %while.35 = (s32[]{:T(128)}, f32[13,8,8,8,13]{3,2,1,4,0:T(8,128)}, f32[13,8,8,8,13]{3,2,1,4,0:T(8,128)}, s32[13]{0:T(128)S(1)}, bf16[20,20,512]{2,1,0:T(8,128)(2...) while((s32[]{:T(128)}, f32[13,8,8,8,13]{3,2,1,4,0:T(8,128)}, ...), condition=%wide.region_3.4_spmd, body=%wide.region_2.3_spmd.sunk | while | flops 2608145 | bytes 11252723 | solution.py:62
  479.7 3.5 fusion.76
  487.4 3.7 multiply_convert_fusion
  492.9 1125.7 %while.36 = (s32[]{:T(128)}, f32[8,8,8,64]{3,2,1,0:T(8,128)}, f32[8,8,8,64]{3,2,1,0:T(8,128)}, f32[20,20,512]{2,1,0:T(8,128)}, f32[20,20,512]{2,1,0:T(8,128)S(1)...) while((s32[]{:T(128)}, f32[8,8,8,64]{3,2,1,0:T(8,128)}, ...), condition=%wide.region_8.9_spmd.clone, body=%wide.region_7.8_spmd.clone.sunk | while | flops 5682196 | bytes 31673668 | solution.py:105
  519.0 2.9 convert_multiply_fusion.55
  555.6 3.1 fusion.139
  576.5 3.1 fusion.137
  605.5 2.9 convert_multiply_fusion.55
  642.1 3.2 fusion.139
  663.1 3.2 fusion.137
  692.1 2.9 convert_multiply_fusion.55
  728.7 3.2 fusion.139
  749.6 3.2 fusion.137
  778.7 2.9 convert_multiply_fusion.55
  815.3 3.2 fusion.139
  836.2 3.2 fusion.137
  901.8 3.2 fusion.139
  922.8 3.2 fusion.137
  988.4 3.2 fusion.139
  1009.4 3.2 fusion.137
  1075.0 3.2 fusion.139
  1096.0 3.2 fusion.137
  1125.0 2.9 convert_multiply_fusion.55
  1161.6 3.2 fusion.139
  1182.5 3.2 fusion.137
  1211.6 2.9 convert_multiply_fusion.55
  1248.1 3.2 fusion.139
  1269.1 3.2 fusion.137
  1298.2 2.9 convert_multiply_fusion.55
  1334.7 3.2 fusion.139
  1355.7 3.2 fusion.137
  1421.3 3.2 fusion.139
  1442.3 3.2 fusion.137
  1507.9 3.2 fusion.139
  1528.8 3.2 fusion.137
  1557.9 2.9 convert_multiply_fusion.55
  1594.4 3.2 fusion.139
  1615.4 3.2 fusion.137
  1622.8 13.0 collective-permute-done.4
  1638.6 11.4 collective-permute-done.5
  1651.0 5.9 collective-permute-start.6
  1663.3 9.5 collective-permute-done.7
  (2407 shorter events, 1112.2 us)
Async XLA Ops:
  7.2 95.6 %copy-start = (bf16[8,8,276]{2,1,0:T(8,128)(2,1)S(1)}, bf16[8,8,276]{2,1,0:T(8,128)(2,1)}, u32[]{:S(2)}) copy-start(bf16[8,8,276]{2,1,0:T(8,128)(2,1)} %param.19) | copy-start | bytes 105988
  7.2 340.4 %copy-start.40 = (bf16[8,8,1024]{2,1,0:T(8,128)(2,1)S(1)}, bf16[8,8,1024]{2,1,0:T(8,128)(2,1)}, u32[]{:S(2)}) copy-start(bf16[8,8,1024]{2,1,0:T(8,128)(2,1)} %param.25) | copy-start | bytes 393220
  7.2 96.4 %all-gather.5.cloned.1.call-start = ((), (), s32[]{:S(2)}) async-start(), calls=%async_computation | async-start | bytes 1064960 | tf_op jit(solution)/shard_map/all_gather | solution.py:132
  7.9 174.3 %all-gather.7.cloned.1.call-start = ((), (), s32[]{:S(2)}) async-start(), calls=%async_computation.1 | async-start | bytes 1064960 | tf_op jit(solution)/shard_map/all_gather | solution.py:133
  8.7 256.3 %all-gather.9.cloned.1.call-start = ((), (), s32[]{:S(2)}) async-start(), calls=%async_computation.2 | async-start | bytes 1064960 | tf_op jit(solution)/shard_map/all_gather | solution.py:131
  9.4 338.2 %all-gather.11.cloned.1.call-start = ((), (), s32[]{:S(2)}) async-start(), calls=%async_computation.3 | async-start | bytes 1064960 | tf_op jit(solution)/shard_map/all_gather | solution.py:134
  102.5 162.5 %copy-start.38 = (bf16[276,1024]{0,1:T(8,128)(2,1)}, bf16[276,1024]{0,1:T(8,128)(2,1)S(1)}, u32[]{:S(2)}) copy-start(bf16[276,1024]{0,1:T(8,128)(2,1)S(1)} %all_gather.15) | copy-start | bytes 1695748
  102.7 246.9 %copy-start.44 = (f32[64]{0:T(128)}, f32[64]{0:T(128)S(1)}, u32[]{:S(2)}) copy-start(f32[64]{0:T(128)S(1)} %mul.75) | copy-start | bytes 772
  103.2 246.1 %copy-start.7 = (f32[64,1024]{1,0:T(8,128)}, f32[64,1024]{1,0:T(8,128)S(1)}, u32[]{:S(2)}) copy-start(f32[64,1024]{1,0:T(8,128)S(1)} %get-tuple-element.505) | copy-start | bytes 786436
  103.3 86.7 %copy-start.42 = (f32[64]{0:T(128)}, f32[64]{0:T(128)S(1)}, u32[]{:S(2)}) copy-start(f32[64]{0:T(128)S(1)} %broadcast_multiply_fusion.2) | copy-start | bytes 772
  103.5 86.5 %copy-start.46 = (f32[64]{0:T(128)}, f32[64]{0:T(128)S(1)}, u32[]{:S(2)}) copy-start(f32[64]{0:T(128)S(1)} %add_rsqrt_fusion) | copy-start | bytes 772
  184.0 82.8 %collective-permute-start = (bf16[2,8,6,512]{3,2,1,0:T(8,128)(2,1)S(1)}, bf16[2,8,6,512]{3,2,1,0:T(8,128)(2,1)S(1)}, u32[]{:S(2)}, u32[]{:S(2)}) collective-permute-start(bf16[2,8,6,512]{3,2,1,0:T(8,128)(2,1)S(1)} %get-tuple-element.489), channel_id=1, source_target_pairs={{0,8},{8,16},{16,24},{24,32},{32,40},{40,48},{48,56},{56,64},{64,7... | collective-permute-start | bytes 294920 | tf_op jit(solution)/shard_map/ppermute | solution.py:20
  188.0 78.8 %collective-permute-start.1 = (bf16[2,8,6,512]{3,2,1,0:T(8,128)(2,1)S(1)}, bf16[2,8,6,512]{3,2,1,0:T(8,128)(2,1)S(1)}, u32[]{:S(2)}, u32[]{:S(2)}) collective-permute-start(bf16[2,8,6,512]{3,2,1,0:T(8,128)(2,1)S(1)} %get-tuple-element.490), channel_id=1, source_target_pairs={{8,0},{16,8},{24,16},{32,24},{40,32},{48,40},{56,48},{64,56},{72,6... | collective-permute-start | bytes 294920 | tf_op jit(solution)/shard_map/ppermute | solution.py:23
  267.0 82.3 %collective-permute-start.2 = (bf16[2,6,20,512]{3,2,1,0:T(8,128)(2,1)S(1)}, bf16[2,6,20,512]{3,2,1,0:T(8,128)(2,1)S(1)}, u32[]{:S(2)}, u32[]{:S(2)}) collective-permute-start(bf16[2,6,20,512]{3,2,1,0:T(8,128)(2,1)S(1)} %get-tuple-element.487), channel_id=1, source_target_pairs={{0,1},{1,2},{2,3},{3,4},{4,5},{5,6},{6,7},{7,0},{8,9},{9,10},{10,1... | collective-permute-start | bytes 737288 | tf_op jit(solution)/shard_map/ppermute | solution.py:20
  269.3 80.0 %collective-permute-start.3 = (bf16[2,6,20,512]{3,2,1,0:T(8,128)(2,1)S(1)}, bf16[2,6,20,512]{3,2,1,0:T(8,128)(2,1)S(1)}, u32[]{:S(2)}, u32[]{:S(2)}) collective-permute-start(bf16[2,6,20,512]{3,2,1,0:T(8,128)(2,1)S(1)} %get-tuple-element.488), channel_id=1, source_target_pairs={{1,0},{2,1},{3,2},{4,3},{5,4},{6,5},{7,6},{0,7},{9,8},{10,9},{11,1... | collective-permute-start | bytes 737288 | tf_op jit(solution)/shard_map/ppermute | solution.py:23
  635.3 27.8 %copy-start.10 = (f32[8,8,8]{2,1,0:T(8,128)S(1)}, f32[8,8,8]{2,1,0:T(8,128)}, u32[]{:S(2)}) copy-start(f32[8,8,8]{2,1,0:T(8,128)} %copy-done.9) | copy-start | bytes 6148 | tf_op jit(solution)/shard_map/while
  635.3 27.8 %copy-start.12 = (f32[8,8,8]{2,1,0:T(8,128)S(1)}, f32[8,8,8]{2,1,0:T(8,128)}, u32[]{:S(2)}) copy-start(f32[8,8,8]{2,1,0:T(8,128)} %copy-done.11) | copy-start | bytes 6148 | tf_op jit(solution)/shard_map/while
  635.3 27.8 %copy-start.14 = (f32[8,8,8]{2,1,0:T(8,128)S(1)}, f32[8,8,8]{2,1,0:T(8,128)}, u32[]{:S(2)}) copy-start(f32[8,8,8]{2,1,0:T(8,128)} %copy-done.13) | copy-start | bytes 6148 | tf_op jit(solution)/shard_map/while
  721.8 27.8 %copy-start.10 = (f32[8,8,8]{2,1,0:T(8,128)S(1)}, f32[8,8,8]{2,1,0:T(8,128)}, u32[]{:S(2)}) copy-start(f32[8,8,8]{2,1,0:T(8,128)} %copy-done.9) | copy-start | bytes 6148 | tf_op jit(solution)/shard_map/while
  721.8 27.8 %copy-start.12 = (f32[8,8,8]{2,1,0:T(8,128)S(1)}, f32[8,8,8]{2,1,0:T(8,128)}, u32[]{:S(2)}) copy-start(f32[8,8,8]{2,1,0:T(8,128)} %copy-done.11) | copy-start | bytes 6148 | tf_op jit(solution)/shard_map/while
  721.8 27.8 %copy-start.14 = (f32[8,8,8]{2,1,0:T(8,128)S(1)}, f32[8,8,8]{2,1,0:T(8,128)}, u32[]{:S(2)}) copy-start(f32[8,8,8]{2,1,0:T(8,128)} %copy-done.13) | copy-start | bytes 6148 | tf_op jit(solution)/shard_map/while
  808.4 27.8 %copy-start.12 = (f32[8,8,8]{2,1,0:T(8,128)S(1)}, f32[8,8,8]{2,1,0:T(8,128)}, u32[]{:S(2)}) copy-start(f32[8,8,8]{2,1,0:T(8,128)} %copy-done.11) | copy-start | bytes 6148 | tf_op jit(solution)/shard_map/while
  808.4 27.8 %copy-start.14 = (f32[8,8,8]{2,1,0:T(8,128)S(1)}, f32[8,8,8]{2,1,0:T(8,128)}, u32[]{:S(2)}) copy-start(f32[8,8,8]{2,1,0:T(8,128)} %copy-done.13) | copy-start | bytes 6148 | tf_op jit(solution)/shard_map/while
  895.0 27.8 %copy-start.12 = (f32[8,8,8]{2,1,0:T(8,128)S(1)}, f32[8,8,8]{2,1,0:T(8,128)}, u32[]{:S(2)}) copy-start(f32[8,8,8]{2,1,0:T(8,128)} %copy-done.11) | copy-start | bytes 6148 | tf_op jit(solution)/shard_map/while
  895.0 27.8 %copy-start.14 = (f32[8,8,8]{2,1,0:T(8,128)S(1)}, f32[8,8,8]{2,1,0:T(8,128)}, u32[]{:S(2)}) copy-start(f32[8,8,8]{2,1,0:T(8,128)} %copy-done.13) | copy-start | bytes 6148 | tf_op jit(solution)/shard_map/while
  981.6 27.8 %copy-start.12 = (f32[8,8,8]{2,1,0:T(8,128)S(1)}, f32[8,8,8]{2,1,0:T(8,128)}, u32[]{:S(2)}) copy-start(f32[8,8,8]{2,1,0:T(8,128)} %copy-done.11) | copy-start | bytes 6148 | tf_op jit(solution)/shard_map/while
  981.6 27.8 %copy-start.14 = (f32[8,8,8]{2,1,0:T(8,128)S(1)}, f32[8,8,8]{2,1,0:T(8,128)}, u32[]{:S(2)}) copy-start(f32[8,8,8]{2,1,0:T(8,128)} %copy-done.13) | copy-start | bytes 6148 | tf_op jit(solution)/shard_map/while
  1068.2 27.8 %copy-start.12 = (f32[8,8,8]{2,1,0:T(8,128)S(1)}, f32[8,8,8]{2,1,0:T(8,128)}, u32[]{:S(2)}) copy-start(f32[8,8,8]{2,1,0:T(8,128)} %copy-done.11) | copy-start | bytes 6148 | tf_op jit(solution)/shard_map/while
  1068.2 27.8 %copy-start.14 = (f32[8,8,8]{2,1,0:T(8,128)S(1)}, f32[8,8,8]{2,1,0:T(8,128)}, u32[]{:S(2)}) copy-start(f32[8,8,8]{2,1,0:T(8,128)} %copy-done.13) | copy-start | bytes 6148 | tf_op jit(solution)/shard_map/while
  1154.7 27.8 %copy-start.12 = (f32[8,8,8]{2,1,0:T(8,128)S(1)}, f32[8,8,8]{2,1,0:T(8,128)}, u32[]{:S(2)}) copy-start(f32[8,8,8]{2,1,0:T(8,128)} %copy-done.11) | copy-start | bytes 6148 | tf_op jit(solution)/shard_map/while
  1154.7 27.8 %copy-start.14 = (f32[8,8,8]{2,1,0:T(8,128)S(1)}, f32[8,8,8]{2,1,0:T(8,128)}, u32[]{:S(2)}) copy-start(f32[8,8,8]{2,1,0:T(8,128)} %copy-done.13) | copy-start | bytes 6148 | tf_op jit(solution)/shard_map/while
  1241.3 27.8 %copy-start.12 = (f32[8,8,8]{2,1,0:T(8,128)S(1)}, f32[8,8,8]{2,1,0:T(8,128)}, u32[]{:S(2)}) copy-start(f32[8,8,8]{2,1,0:T(8,128)} %copy-done.11) | copy-start | bytes 6148 | tf_op jit(solution)/shard_map/while
  1241.3 27.8 %copy-start.14 = (f32[8,8,8]{2,1,0:T(8,128)S(1)}, f32[8,8,8]{2,1,0:T(8,128)}, u32[]{:S(2)}) copy-start(f32[8,8,8]{2,1,0:T(8,128)} %copy-done.13) | copy-start | bytes 6148 | tf_op jit(solution)/shard_map/while
  1327.9 27.8 %copy-start.12 = (f32[8,8,8]{2,1,0:T(8,128)S(1)}, f32[8,8,8]{2,1,0:T(8,128)}, u32[]{:S(2)}) copy-start(f32[8,8,8]{2,1,0:T(8,128)} %copy-done.11) | copy-start | bytes 6148 | tf_op jit(solution)/shard_map/while
  1327.9 27.8 %copy-start.14 = (f32[8,8,8]{2,1,0:T(8,128)S(1)}, f32[8,8,8]{2,1,0:T(8,128)}, u32[]{:S(2)}) copy-start(f32[8,8,8]{2,1,0:T(8,128)} %copy-done.13) | copy-start | bytes 6148 | tf_op jit(solution)/shard_map/while
  1414.4 27.8 %copy-start.12 = (f32[8,8,8]{2,1,0:T(8,128)S(1)}, f32[8,8,8]{2,1,0:T(8,128)}, u32[]{:S(2)}) copy-start(f32[8,8,8]{2,1,0:T(8,128)} %copy-done.11) | copy-start | bytes 6148 | tf_op jit(solution)/shard_map/while
  1414.4 27.8 %copy-start.14 = (f32[8,8,8]{2,1,0:T(8,128)S(1)}, f32[8,8,8]{2,1,0:T(8,128)}, u32[]{:S(2)}) copy-start(f32[8,8,8]{2,1,0:T(8,128)} %copy-done.13) | copy-start | bytes 6148 | tf_op jit(solution)/shard_map/while
  1501.0 27.8 %copy-start.12 = (f32[8,8,8]{2,1,0:T(8,128)S(1)}, f32[8,8,8]{2,1,0:T(8,128)}, u32[]{:S(2)}) copy-start(f32[8,8,8]{2,1,0:T(8,128)} %copy-done.11) | copy-start | bytes 6148 | tf_op jit(solution)/shard_map/while
  1501.0 27.8 %copy-start.14 = (f32[8,8,8]{2,1,0:T(8,128)S(1)}, f32[8,8,8]{2,1,0:T(8,128)}, u32[]{:S(2)}) copy-start(f32[8,8,8]{2,1,0:T(8,128)} %copy-done.13) | copy-start | bytes 6148 | tf_op jit(solution)/shard_map/while
  1587.6 27.8 %copy-start.12 = (f32[8,8,8]{2,1,0:T(8,128)S(1)}, f32[8,8,8]{2,1,0:T(8,128)}, u32[]{:S(2)}) copy-start(f32[8,8,8]{2,1,0:T(8,128)} %copy-done.11) | copy-start | bytes 6148 | tf_op jit(solution)/shard_map/while
  1587.6 27.8 %copy-start.14 = (f32[8,8,8]{2,1,0:T(8,128)S(1)}, f32[8,8,8]{2,1,0:T(8,128)}, u32[]{:S(2)}) copy-start(f32[8,8,8]{2,1,0:T(8,128)} %copy-done.13) | copy-start | bytes 6148 | tf_op jit(solution)/shard_map/while
  1620.3 38.2 %copy-start.5 = (f32[8,8,8,64]{3,2,1,0:T(8,128)S(1)}, f32[8,8,8,64]{3,2,1,0:T(8,128)}, u32[]{:S(2)}) copy-start(f32[8,8,8,64]{3,2,1,0:T(8,128)} %get-tuple-element.247) | copy-start | bytes 393220
  1620.3 15.5 collective-permute-start.4
  1622.8 35.9 %copy-start.8 = (f32[64,1024]{1,0:T(8,128)S(1)}, f32[64,1024]{1,0:T(8,128)}, u32[]{:S(2)}) copy-start(f32[64,1024]{1,0:T(8,128)} %copy-done.7) | copy-start | bytes 786436
  1622.8 35.9 %copy-start.45 = (f32[64]{0:T(128)S(1)}, f32[64]{0:T(128)}, u32[]{:S(2)}) copy-start(f32[64]{0:T(128)} %copy-done.44) | copy-start | bytes 772
  1636.5 13.6 collective-permute-start.5
  1651.0 11.9 collective-permute-start.6
  1661.1 11.7 collective-permute-start.7
  (360 other events, 1565.4 us)
Sparse Core Ops, SparseCore 0:
  11.4 88.1 all-gather.4
  102.9 79.2 all-gather.6
  185.6 79.3 all-gather.8
  268.2 79.3 all-gather.10
where the time goes:
time: 1700 us; the launch traced here: 1680 us
  local copies, waits for them, and re-layouts  925 us (54%)
  other arithmetic  271 us (16%)
  waiting for transfers between devices  263 us (15%)
  blocking collectives  92.5 us (5%)
  loops' own time  77.9 us (5%)
  starting transfers between devices  24.6 us (1%)
    dot_general x338, local copies, waits for them, and re-layouts, head_scale(): jnp.einsum('rch,rche->rche', weight, grid, preferred_element_type=jnp.flo...  427 us
    reshape x169, local copies, waits for them, and re-layouts, second(): head_scale(p_row[..., offset], g_heads)  194 us
    reshape x169, local copies, waits for them, and re-layouts, second(): head_scale(s_row[..., offset], q_heads)  186 us
    dot_general x39, other arithmetic, head_scale(): jnp.einsum('rch,rche->rche', weight, grid, preferred_element_type=jnp.flo...  96.7 us
    all_gather x1, blocking collectives, body(): lax.all_gather(embed_weight, 'lon', axis=1, tiled=True)  92.5 us
    all_gather x1, waiting for transfers between devices, body(): lax.all_gather(value_weight, 'lon', axis=1, tiled=True)  77 us
    all_gather x1, waiting for transfers between devices, body(): lax.all_gather(query_weight, 'lon', axis=1, tiled=True)  75 us
    all_gather x1, waiting for transfers between devices, body(): lax.all_gather(out_weight, 'lon', axis=1, tiled=True)  74.2 us
  transfers between devices with their start and end apart: 12, of which 6 were waited for; matrix products, arithmetic and copies ran while one was open for 1% of the time, Pallas kernels for 0%

commit v1 on v0

v1 whole, which is shorter than its diff:
```python
import functools
import math

import jax
import jax.numpy as jnp
from jax import lax
from jax.experimental import pallas as pl
from jax.experimental.pallas import tpu as pltpu
from jax.sharding import PartitionSpec as P

HEADS = 8
RAD = 6
PAD = 6
EPS = 1e-05
MESH = pl.DeviceIdType.MESH
F32 = jnp.float32
BF16 = jnp.bfloat16

SIDE = 8
OWN = SIDE * SIDE
RIM = RAD * SIDE
BAND = OWN + 2 * RIM
EXT = 3 * BAND
HERE = BAND + RIM

NT = (((1,), (1,)), ((), ()))
NN = (((1,), (0,)), ((), ()))


def dot_nt(left, right):
    return lax.dot_general(left, right, NT, preferred_element_type=F32)


def dot_nn(left, right):
    return lax.dot_general(left, right, NN, preferred_element_type=F32)


def kernel(
    sizes, p_ref, q_ref, k_ref, v_ref, o_ref, e_ref, c_ref, out_ref, grad_ref,
    ge, go, gk, gq, gv, wk, wq, wv, px, cx, sx, nx, qx, kx, vx, gx, emb, nor, inv, att, dq, dk, dv, bias,
    y_send, y_recv, z_send, z_recv, s_send, s_recv, h_send, h_recv,
):
    lons, lats_dev = sizes
    lon, lat = lax.axis_index("lon"), lax.axis_index("lat")
    core, yh, z = lax.rem(lon, 2), lax.rem(lon // 2, 4), lon // 8
    zs = lons // 8
    first_row = lat * SIDE
    lats = SIDE * lats_dev - PAD
    patch_width = p_ref.shape[1]
    width = c_ref.shape[1]
    half = width // 2

    parts = (ge, go, gk, gq, gv)

    ge[z, yh, core] = jnp.zeros(ge.shape[3:], BF16)
    ge[z, yh, core, :, 0:patch_width] = e_ref[...]
    go[z, yh, core] = o_ref[...]
    for store, source in ((gk, k_ref), (gq, q_ref), (gv, v_ref)):
        wide = source[...].astype(F32)
        store[z, yh, core] = jnp.concatenate([wide[:, :half], wide[:, half:]], axis=0).astype(BF16)
    px[HERE : HERE + OWN] = jnp.zeros((OWN, px.shape[1]), BF16)
    px[HERE : HERE + OWN, 0:patch_width] = p_ref[...]
    cx[HERE : HERE + OWN] = c_ref[...]

    around = [(a, b) for a in (-1, 0, 1) for b in (-1, 0, 1) if (a, b) != (0, 0)]

    def near(a, b):
        return (lax.rem(lon + lons + a, lons), lax.rem(lat + lats_dev + b, lats_dev))

    def at_y(d):
        return ((z * 4 + lax.rem(yh + d, 4)) * 2 + core, lat)

    def at_z(d):
        return ((lax.rem(z + d + zs, zs) * 4 + yh) * 2 + core, lat)

    sibling = (lon + 1 - 2 * core, lat)
    greeted = [near(a, b) for a, b in around] + [at_y(1), at_y(2), at_y(3), at_z(1), at_z(-1), sibling]
    barrier = pltpu.get_barrier_semaphore()
    for partner in greeted:
        pl.semaphore_signal(barrier, inc=1, device_id=partner, device_id_type=MESH)
    pl.semaphore_wait(barrier, len(greeted))

    def send(source, target, send_sem, recv_sem, partner):
        copy = pltpu.make_async_remote_copy(
            src_ref=source, dst_ref=target, send_sem=send_sem, recv_sem=recv_sem,
            device_id=partner, device_id_type=MESH,
        )
        copy.start()
        return copy

    sent = []

    first = []
    for w, part in enumerate(parts):
        block = part.at[z, yh, core]
        first.append([
            send(block, block, y_send.at[w, d - 1], y_recv.at[w, d - 1], at_y(d)) for d in (1, 2, 3)
        ])
        sent.extend(first[-1])

    def pieces(b):
        if b == 1:
            return (OWN - RIM, RIM, 0)
        if b == -1:
            return (0, RIM, RIM + OWN)
        return (0, OWN, RIM)

    def spread(store, which):
        copies = []
        for n, (a, b) in enumerate(around):
            begin, count, place = pieces(b)
            copies.append(send(
                store.at[pl.ds(HERE + begin, count)],
                store.at[pl.ds((1 - a) * BAND + place, count)],
                h_send.at[which, n], h_recv.at[which, n], near(a, b),
            ))
        return copies

    cells = spread(px, 0) + spread(cx, 1)

    def steps_of(w, way):
        return zs // 2 if (w + way) % 2 == 0 else zs // 2 - 1

    ring = {}
    for step in range(1, zs // 2 + 1):
        for w, part in enumerate(parts):
            if step == 1:
                for copy in first[w]:
                    copy.wait_recv()
            for way, d in ((0, 1), (1, -1)):
                if step > 1 and step - 1 <= steps_of(w, way):
                    ring[w, way, step - 1].wait_recv()
                if step <= steps_of(w, way):
                    lines = part.at[lax.rem(z - d * (step - 1) + zs, zs), :, core]
                    ring[w, way, step] = send(
                        lines, lines, z_send.at[w, way, step - 1], z_recv.at[w, way, step - 1], at_z(d)
                    )
                    sent.append(ring[w, way, step])

    cell = lax.broadcasted_iota(jnp.int32, (OWN, EXT), 0)
    other = lax.broadcasted_iota(jnp.int32, (OWN, EXT), 1)
    band = jnp.where(other >= BAND, 1, 0) + jnp.where(other >= 2 * BAND, 1, 0)
    rows = ((other - band * BAND) >> 3) - (cell >> 3)
    cols = (band - 1) * SIDE + (other & 7) - (cell & 7)
    inside = (rows >= 0) & (rows <= 2 * RAD) & (cols >= -RAD) & (cols <= RAD)
    other_row = ((other - band * BAND) >> 3) - RAD + first_row
    cell_row = (cell >> 3) + first_row
    bias[0] = jnp.where(inside & (other_row >= 0) & (other_row < lats), 0.0, -jnp.inf).astype(F32)
    bias[1] = jnp.where(
        inside & (cell_row < lats) & (other_row >= 0) & (other_row < SIDE * lats_dev), 0.0, -jnp.inf
    ).astype(F32)

    def finish(w):
        part = parts[w]
        for way in (0, 1):
            if steps_of(w, way) == zs // 2:
                ring[w, way, zs // 2].wait_recv()
        copy = send(part.at[:, :, core], part.at[:, :, core], s_send.at[w], s_recv.at[w], sibling)
        sent.append(copy)
        return copy

    swaps = [finish(w) for w in range(len(parts))]
    for copy in cells:
        copy.wait_recv()

    scale = 1.0 / math.sqrt(wq.shape[0] // HEADS)
    pairs = HEADS // 2
    bands = [slice(n * BAND, (n + 1) * BAND) for n in range(3)]
    here = slice(HERE, HERE + OWN)

    swaps[0].wait_recv()
    for n, rows_of in enumerate(bands):
        raw = dot_nt(px[rows_of], ge[...].reshape(width, ge.shape[-1]))
        centred = raw - jnp.mean(raw, axis=-1, keepdims=True)
        inverse = lax.rsqrt(jnp.mean(centred * centred, axis=-1, keepdims=True) + EPS)
        normal = centred * inverse
        nx[rows_of] = normal.astype(BF16)
        if n == 1:
            emb[...] = raw[RIM : RIM + OWN]
            nor[...] = normal[RIM : RIM + OWN]
            inv[...] = jnp.broadcast_to(inverse[RIM : RIM + OWN], inv.shape)

    swaps[1].wait_recv()
    ext_row = lax.broadcasted_iota(jnp.int32, (BAND, 1), 0) // SIDE - RAD + first_row
    valid = jnp.where(ext_row < lats, 1.0, 0.0).astype(F32)
    for rows_of in bands:
        grad = dot_nn(cx[rows_of], go[...].reshape(width, go.shape[-1]))
        gx[rows_of] = (grad * valid).astype(BF16)

    for w, weight, result in ((2, wk, kx), (3, wq, qx), (4, wv, vx)):
        swaps[w].wait_recv()

        def order(i, carry, part=parts[w], weight=weight):
            lines = part[i].astype(F32).reshape(8, 2, 8, half)
            begin = pl.ds(pl.multiple_of(i * 64, 64), 64)
            weight[begin, 0:half] = lines[:, 0].reshape(64, half).astype(BF16)
            weight[begin, half:] = lines[:, 1].reshape(64, half).astype(BF16)
            return carry

        lax.fori_loop(0, zs, order, 0)
        for rows_of in bands:
            result[rows_of] = dot_nt(nx[rows_of], weight[...]).astype(BF16)

    low = lax.broadcasted_iota(jnp.int32, (OWN, 128), 1) < 64
    none = jnp.zeros((OWN, 128), BF16)

    def apart(tile):
        return jnp.concatenate([jnp.where(low, tile, none), jnp.where(low, none, tile)], axis=0)

    def together(both):
        return jnp.where(low, both[:OWN], both[OWN:])

    lane = lax.broadcasted_iota(jnp.int32, (OWN, 128), 1)
    known = jnp.zeros((OWN, 128), F32)
    reach = jnp.concatenate([bias[0], bias[0]], axis=0)
    for p in range(pairs):
        tile = slice(p * 128, (p + 1) * 128)
        keys, values = kx[:, tile], vx[:, tile]
        scores = dot_nt(apart(qx[here, tile]), keys) * scale + reach
        top = jnp.max(scores, axis=-1, keepdims=True)
        terms = jnp.exp(scores - top)
        total = jnp.sum(terms, axis=-1, keepdims=True)
        prob = terms / total
        dprob = dot_nt(apart(gx[here, tile]), values)
        delta = jnp.sum(prob * dprob, axis=-1, keepdims=True)
        dscore = (prob * (dprob - delta)).astype(BF16)
        att[:, tile] = together(dot_nn(prob.astype(BF16), values)).astype(BF16)
        dq[:, tile] = together(dot_nn(dscore, keys) * scale).astype(BF16)
        for place, column in ((0, top), (HEADS, total), (2 * HEADS, delta)):
            known = jnp.where(lane == place + 2 * p, column[:OWN], known)
            known = jnp.where(lane == place + 2 * p + 1, column[OWN:], known)

    sx[here] = known
    told = spread(sx, 2)
    mixed = emb[...] + dot_nt(att[...], go[...].reshape(width, go.shape[-1]))
    own_row = lax.broadcasted_iota(jnp.int32, (OWN, 1), 0) // SIDE + first_row
    own_valid = jnp.where(own_row < lats, 1.0, 0.0).astype(F32)
    out_ref[...] = (mixed * own_valid).astype(BF16)
    for copy in told:
        copy.wait_recv()

    facts = jnp.transpose(sx[...], (1, 0))
    reach = jnp.concatenate([bias[1], bias[1]], axis=0)
    for p in range(pairs):
        tile = slice(p * 128, (p + 1) * 128)

        def fact(place):
            first = jnp.broadcast_to(facts[place + 2 * p : place + 2 * p + 1, :EXT], (OWN, EXT))
            second = jnp.broadcast_to(facts[place + 2 * p + 1 : place + 2 * p + 2, :EXT], (OWN, EXT))
            return jnp.concatenate([first, second], axis=0)

        queries, grads = qx[:, tile], gx[:, tile]
        scores = dot_nt(apart(kx[here, tile]), queries) * scale + reach
        prob = jnp.exp(scores - fact(0)) / fact(HEADS)
        dprob = dot_nt(apart(vx[here, tile]), grads)
        dscore = (prob * (dprob - fact(2 * HEADS))).astype(BF16)
        dk[:, tile] = together(dot_nn(dscore, queries) * scale).astype(BF16)
        dv[:, tile] = together(dot_nn(prob.astype(BF16), grads)).astype(BF16)

    slope = dot_nn(dq[...], wq[...]) + dot_nn(dk[...], wk[...]) + dot_nn(dv[...], wv[...])
    normal = nor[...]
    centre = jnp.mean(slope, axis=-1, keepdims=True)
    along = jnp.mean(slope * normal, axis=-1, keepdims=True)
    masked = c_ref[...].astype(F32) * own_valid
    grad_embed = (masked + inv[:, 0:1] * (slope - centre - normal * along)).astype(BF16)
    result = dot_nn(grad_embed, ge[...].reshape(width, ge.shape[-1])).astype(BF16)
    grad_ref[...] = result[:, 0:patch_width]

    for copy in sent + cells + told:
        copy.wait_send()


def body(patches, query_weight, key_weight, value_weight, out_weight, embed_weight, cotangent):
    rows, cols, patch_width = patches.shape
    width = cotangent.shape[-1]
    lons, lats_dev = lax.axis_size("lon"), lax.axis_size("lat")
    zs = lons // 8
    channels = query_weight.shape[1] * lons
    wide_patch = -(-patch_width // 128) * 128
    blocks = (zs, 4, 2, 16)
    vmem = pltpu.VMEM
    dma = pltpu.SemaphoreType.DMA
    out, grad = pl.pallas_call(
        functools.partial(kernel, (lons, lats_dev)),
        out_shape=(
            jax.ShapeDtypeStruct((OWN, width), BF16),
            jax.ShapeDtypeStruct((OWN, patch_width), BF16),
        ),
        in_specs=[pl.BlockSpec(memory_space=vmem)] * 7,
        out_specs=(pl.BlockSpec(memory_space=vmem),) * 2,
        scratch_shapes=[
            vmem(blocks + (wide_patch,), BF16),
            vmem(blocks + (channels,), BF16),
            vmem(blocks + (width // 2,), BF16),
            vmem(blocks + (width // 2,), BF16),
            vmem(blocks + (width // 2,), BF16),
            vmem((channels, width), BF16),
            vmem((channels, width), BF16),
            vmem((channels, width), BF16),
            vmem((EXT, wide_patch), BF16),
            vmem((EXT, width), BF16),
            vmem((512, 128), F32),
            vmem((EXT, width), BF16),
            vmem((EXT, channels), BF16),
            vmem((EXT, channels), BF16),
            vmem((EXT, channels), BF16),
            vmem((EXT, channels), BF16),
            vmem((OWN, width), F32),
            vmem((OWN, width), F32),
            vmem((OWN, 128), F32),
            vmem((OWN, channels), BF16),
            vmem((OWN, channels), BF16),
            vmem((OWN, channels), BF16),
            vmem((OWN, channels), BF16),
            vmem((2, OWN, EXT), F32),
            dma((5, 3)),
            dma((5, 3)),
            dma((5, 2, zs // 2)),
            dma((5, 2, zs // 2)),
            dma((5,)),
            dma((5,)),
            dma((3, 8)),
            dma((3, 8)),
        ],
        compiler_params=pltpu.CompilerParams(
            collective_id=0, has_side_effects=True, vmem_limit_bytes=48 * 1024 * 1024
        ),
    )(
        patches.reshape(rows * cols, patch_width),
        query_weight.T,
        key_weight.T,
        value_weight.T,
        out_weight.T,
        embed_weight.T,
        cotangent.reshape(rows * cols, width),
    )
    return out.reshape(rows, cols, width), grad.reshape(rows, cols, patch_width)


def solution(mesh):
    in_specs = (
        P("lat", "lon", None),
        P(None, "lon"),
        P(None, "lon"),
        P(None, "lon"),
        P(None, "lon"),
        P(None, "lon"),
        P("lat", "lon", None),
    )
    out_specs = (P("lat", "lon", None), P("lat", "lon", None))
    return jax.shard_map(body, mesh=mesh, in_specs=in_specs, out_specs=out_specs, check_vma=False)
```

time: 1700 us -> 75.8 us (0.04)
  the two profiles are of different devices: /device:TPU:3 before, /device:TPU:1 now
where the time goes in v1:
time: 75.8 us; the launch traced here: 75.2 us
  Pallas kernels  68 us (90%)
  local copies, waits for them, and re-layouts  6.55 us (9%)
    pallas_call x1, Pallas kernels, body(): pl.pallas_call(functools.partial(kernel, (lons, lats_dev)), out_shape=(ja...  68 us
    unnamed x16, local copies, waits for them, and re-layouts  6.55 us

profile of v1, /device:TPU:1, one launch (start us, length us, event | category | flops | bytes accessed | tf_op | source)
XLA Modules:
  0.0 75.2 jit_solution(14206193791529943793)
XLA Ops:
  0.6 0.0 copy-start.6
  0.6 0.7 copy-done.6
  1.3 0.0 copy-start
  1.3 0.9 %copy-done = bf16[8,8,1024]{2,1,0:T(8,128)(2,1)S(1)} copy-done((bf16[8,8,1024]{2,1,0:T(8,128)(2,1)S(1)}, bf16[8,8,1024]{2,1,0:T(8,128)(2,1)}, u32[]{:S(2)}) %copy-start) | copy-done | bytes 131096
  2.2 0.0 copy-start.1
  2.2 0.8 %copy-done.1 = bf16[8,8,276]{2,1,0:T(8,128)(2,1)S(1)} copy-done((bf16[8,8,276]{2,1,0:T(8,128)(2,1)S(1)}, bf16[8,8,276]{2,1,0:T(8,128)(2,1)}, u32[]{:S(2)}) %copy-start.1) | copy-done | bytes 35352
  3.0 0.0 copy-start.2
  3.0 0.7 copy-done.2
  3.8 0.0 copy-start.3
  3.8 0.7 copy-done.3
  4.5 0.0 copy-start.4
  4.5 0.7 copy-done.4
  5.2 0.0 copy-start.5
  5.2 0.7 copy-done.5
  5.9 68.0 %shard_map.86 = (bf16[64,1024]{1,0:T(8,128)(2,1)S(1)}, bf16[64,276]{1,0:T(8,128)(2,1)S(1)}) custom-call(bf16[64,276]{1,0:T(8,128)(2,1)S(1)} %bitcast.12, bf16[8,1024]{1,0:T(8,128)(2,1)S(1)} %bitcast.13, bf16[8,1024]{1,0:T(8,128)(2,1)S(1)} %bitcast.14, bf16[8,1024]{1,0:T(8,128)(2,1)S(1)} %bitcast.15, bf16[16,512]{1,0:T(8,128)(2,1)S(1)} %bitcast.16, ...), custom_call_target="tpu_custom_call" | custom-call | tf_op jit(solution)/shard_map/pallas_call | solution.py:283
  74.0 0.7 copy.11
  74.6 0.6 copy.12
Async XLA Ops:
  0.6 0.7 copy-start.6
  1.3 0.9 %copy-start = (bf16[8,8,1024]{2,1,0:T(8,128)(2,1)S(1)}, bf16[8,8,1024]{2,1,0:T(8,128)(2,1)}, u32[]{:S(2)}) copy-start(bf16[8,8,1024]{2,1,0:T(8,128)(2,1)} %param.13) | copy-start | bytes 393220
  2.2 0.8 %copy-start.1 = (bf16[8,8,276]{2,1,0:T(8,128)(2,1)S(1)}, bf16[8,8,276]{2,1,0:T(8,128)(2,1)}, u32[]{:S(2)}) copy-start(bf16[8,8,276]{2,1,0:T(8,128)(2,1)} %param.7) | copy-start | bytes 105988
  3.0 0.7 copy-start.2
  3.8 0.7 copy-start.3
  4.5 0.7 copy-start.4
  5.2 0.7 copy-start.5

commit v2 on v1

v2 whole, which is shorter than its diff:
```python
import functools
import math

import jax
import jax.numpy as jnp
from jax import lax
from jax.experimental import pallas as pl
from jax.experimental.pallas import tpu as pltpu
from jax.sharding import PartitionSpec as P

HEADS = 8
RAD = 6
PAD = 6
EPS = 1e-05
MESH = pl.DeviceIdType.MESH
F32 = jnp.float32
BF16 = jnp.bfloat16

SIDE = 8
OWN = SIDE * SIDE
RIM = RAD * SIDE
BAND = OWN + 2 * RIM
EXT = 3 * BAND
HERE = BAND + RIM

NT = (((1,), (1,)), ((), ()))
NN = (((1,), (0,)), ((), ()))


def dot_nt(left, right):
    return lax.dot_general(left, right, NT, preferred_element_type=F32)


def dot_nn(left, right):
    return lax.dot_general(left, right, NN, preferred_element_type=F32)


WHOLE = ("e",)
SPLIT = ("k", "v", "q", "o")


def kernel(
    sizes, p_ref, q_ref, k_ref, v_ref, o_ref, e_ref, c_ref, out_ref, grad_ref,
    whole, gb, raw8, raw16, rawp, stage, wk, wq, wv, px, cx, sx, nx, qx, kx, vx, gx, emb, nor, inv, att, dq, dk, dv, bias,
    y_send, y_recv, z_send, z_recv, x_send, x_recv, s_send, s_recv, h_send, h_recv, f_send, f_recv, l_sem,
):
    lons, lats_dev = sizes
    lon, lat = lax.axis_index("lon"), lax.axis_index("lat")
    core, yh, z = lax.rem(lon, 2), lax.rem(lon // 2, 4), lon // 8
    x, yl = lat // 2, lax.rem(lat, 2)
    zs, xs = lons // 8, lats_dev // 2
    first_row = lat * SIDE
    lats = SIDE * lats_dev - PAD
    patch_width = p_ref.shape[1]
    width = c_ref.shape[1]
    half = width // 2
    quarter = gb.shape[-1] // xs

    around = [(a, b) for a in (-1, 0, 1) for b in (-1, 0, 1) if (a, b) != (0, 0)]

    def near(a, b):
        return (lax.rem(lon + lons + a, lons), lax.rem(lat + lats_dev + b, lats_dev))

    def at_y(d):
        y = lax.rem(2 * yh + yl + 8 + (2 * yl - 1) * d, 8)
        return ((z * 4 + y // 2) * 2 + core, 2 * x + lax.rem(y, 2))

    def at_z(d):
        return ((lax.rem(z + d + zs, zs) * 4 + yh) * 2 + core, lat)

    def at_x(d):
        return (lon, 2 * lax.rem(x + d + xs, xs) + yl)

    sibling = (lon + 1 - 2 * core, lat)
    greeted = [near(a, b) for a, b in around] + [at_y(1), at_y(2), at_y(-2), at_y(3)]
    greeted += [at_z(1), at_z(-1), at_x(1), at_x(-1), at_x(2), sibling]
    barrier = pltpu.get_barrier_semaphore()
    for partner in greeted:
        pl.semaphore_signal(barrier, inc=1, device_id=partner, device_id_type=MESH)

    here = slice(HERE, HERE + OWN)
    local = [
        pltpu.make_async_copy(source, target, l_sem.at[n])
        for n, (source, target) in enumerate((
            (q_ref, raw8.at[0]), (k_ref, raw8.at[1]), (v_ref, raw8.at[2]),
            (o_ref, raw16), (e_ref, rawp[1]),
            (p_ref, rawp[0]), (c_ref, cx.at[pl.ds(HERE, OWN)]),
        ))
    ]
    for copy in local:
        copy.start()

    for copy in local:
        copy.wait()

    def lanes(d):
        return pl.ds(pl.multiple_of(lax.rem(x + d + xs, xs) * quarter, 128), quarter)

    def folded(n):
        wide = raw8[n].astype(F32)
        return jnp.concatenate([wide[:, :half], wide[:, half:]], axis=0).astype(BF16)

    pads = whole[0].shape[-1]
    whole[0][z, yh, core] = jnp.zeros((16, pads), BF16)
    whole[0][z, yh, core, :, 0:patch_width] = rawp[1][...]
    for n, name in enumerate(SPLIT):
        stage[n] = raw16[...] if name == "o" else folded("qkv".index(name))
    gb[z, yh, core, :, lanes(0)] = stage[x]
    px[here] = jnp.zeros((OWN, px.shape[1]), BF16)
    px[here, 0:patch_width] = rawp[0][...]

    pl.semaphore_wait(barrier, len(greeted))

    sent = []

    def send(source, target, send_sem, recv_sem, partner):
        copy = pltpu.make_async_remote_copy(
            src_ref=source, dst_ref=target, send_sem=send_sem, recv_sem=recv_sem,
            device_id=partner, device_id_type=MESH,
        )
        copy.start()
        sent.append(copy)
        return copy

    order = ("b", 0)
    last = len(order) - 1
    soon = 5

    def lines(part, at):
        return gb.at[at, :, core, :, lanes(0)] if part == "b" else whole[part].at[at, :, core]

    def place_of(way, step):
        return lax.rem(z - (1, -1)[way] * step + zs, zs)

    first = {}
    for i, part in enumerate(order):
        block = gb.at[z, yh, core, :, lanes(0)] if part == "b" else whole[part].at[z, yh, core]
        first[i] = [send(block, block, y_send.at[i, d - 1], y_recv.at[i, d - 1], at_y(d)) for d in (1, 2, 3)]

    def steps_of(i, way):
        return zs // 2 if (way == 1) == (i == last) else zs // 2 - 1

    ring, across, ahead, swap = {}, {}, {}, {}

    def go_across(n, at):
        source = gb.at[at, :, core, :, lanes(0)]
        across[n] = [
            send(source, source, x_send.at[n, side], x_recv.at[n, side], at_x(d)) for side, d in ((0, 1), (1, -1))
        ]
        if n >= soon:
            ahead[n] = send(source, source, x_send.at[n, 2], x_recv.at[n, 2], at_x(2))

    def go_ahead(n, at):
        for copy in across[n]:
            copy.wait_recv()
        if n >= soon:
            return
        d = 1 if n % 2 == 0 else -1
        source = gb.at[at, :, core, :, lanes(-d)]
        ahead[n] = send(source, source, x_send.at[n, 2], x_recv.at[n, 2], at_x(d))

    def go_over(part, n, at):
        if part == "b":
            ahead[n].wait_recv()
        source = gb.at[at, :, core] if part == "b" else whole[part].at[at, :, core]
        i = order.index(part)
        swap[part, n] = send(source, source, s_send.at[i, n], s_recv.at[i, n], sibling)

    def came(step, i):
        if step == 1:
            return [(0, z)]
        return [
            (2 * (step - 1) - 1 + way, place_of(way, step - 1)) for way in (0, 1) if step - 1 <= steps_of(i, way)
        ]

    def numbers(step, i):
        return [(n if step < zs // 2 + 1 else zs - 1, at) for n, at in came(step, i)]

    def arrange(n, at):
        swap["b", n].wait_recv()
        for name, weight in (("k", wk), ("q", wq), ("v", wv)):
            begin_lane = half * SPLIT.index(name)
            wide = gb[at, :, :, :, begin_lane : begin_lane + half].astype(F32).reshape(8, 2, 8, half)
            begin = pl.ds(pl.multiple_of(at * 64, 64), 64)
            weight[begin, 0:half] = wide[:, 0].reshape(64, half).astype(BF16)
            weight[begin, half:] = wide[:, 1].reshape(64, half).astype(BF16)

    def slot(step):
        for i, part in enumerate(order):
            if step <= zs // 2 + 1:
                if step == 1:
                    for copy in first[i]:
                        copy.wait_recv()
                for way in (0, 1):
                    if step > 1 and step - 1 <= steps_of(i, way):
                        ring[i, way, step - 1].wait_recv()
                    if step <= steps_of(i, way):
                        source = lines(part, place_of(way, step - 1))
                        ring[i, way, step] = send(
                            source, source, z_send.at[i, way, step - 1], z_recv.at[i, way, step - 1],
                            at_z((1, -1)[way]),
                        )
                for n, at in numbers(step, i):
                    if part == "b":
                        go_across(n, at)
                    else:
                        go_over(part, n, at)
        if 1 <= step - 1 <= zs // 2 + 1:
            for n, at in numbers(step - 1, 0):
                go_ahead(n, at)
                if n >= soon:
                    go_over("b", n, at)
        if 1 <= step - 2 <= zs // 2 + 1:
            for n, at in numbers(step - 2, 0):
                if n < soon:
                    go_over("b", n, at)
        if 1 <= step - 3 <= zs // 2 + 1:
            for n, at in numbers(step - 3, 0):
                if n < soon:
                    arrange(n, at)

    def arrived(part):
        for n in range(zs):
            swap[part, n].wait_recv()

    slot(1)

    def poleward(store, which):
        return [
            send(store.at[pl.ds(HERE + OWN - RIM, RIM)], store.at[pl.ds(BAND, RIM)],
                 h_send.at[which, 0], h_recv.at[which, 0], near(0, 1)),
            send(store.at[pl.ds(HERE, RIM)], store.at[pl.ds(HERE + OWN, RIM)],
                 h_send.at[which, 1], h_recv.at[which, 1], near(0, -1)),
        ]

    def sideward(store, which):
        source = store.at[pl.ds(BAND, BAND)]
        return [
            send(source, store.at[pl.ds(0, BAND)], h_send.at[which, 2], h_recv.at[which, 2], near(1, 0)),
            send(source, store.at[pl.ds(2 * BAND, BAND)], h_send.at[which, 3], h_recv.at[which, 3], near(-1, 0)),
        ]

    halo = poleward(px, 0), poleward(cx, 1)
    cell = lax.broadcasted_iota(jnp.int32, (OWN, EXT), 0)
    other = lax.broadcasted_iota(jnp.int32, (OWN, EXT), 1)
    band = jnp.where(other >= BAND, 1, 0) + jnp.where(other >= 2 * BAND, 1, 0)
    rows = ((other - band * BAND) >> 3) - (cell >> 3)
    cols = (band - 1) * SIDE + (other & 7) - (cell & 7)
    inside = (rows >= 0) & (rows <= 2 * RAD) & (cols >= -RAD) & (cols <= RAD)
    other_row = ((other - band * BAND) >> 3) - RAD + first_row
    cell_row = (cell >> 3) + first_row
    bias[0] = jnp.where(inside & (other_row >= 0) & (other_row < lats), 0.0, -jnp.inf).astype(F32)
    bias[1] = jnp.where(
        inside & (cell_row < lats) & (other_row >= 0) & (other_row < SIDE * lats_dev), 0.0, -jnp.inf
    ).astype(F32)

    slot(2)
    for copy in halo[0] + halo[1]:
        copy.wait_recv()
    halo = sideward(px, 0), sideward(cx, 1)
    for step in range(3, zs // 2 + 2):
        slot(step)

    def embed(n):
        rows_of = slice(n * BAND, (n + 1) * BAND)
        raw = dot_nt(px[rows_of], whole[0][...].reshape(width, pads))
        centred = raw - jnp.mean(raw, axis=-1, keepdims=True)
        inverse = lax.rsqrt(jnp.mean(centred * centred, axis=-1, keepdims=True) + EPS)
        normal = centred * inverse
        nx[rows_of] = normal.astype(BF16)
        if n == 1:
            emb[...] = raw[RIM : RIM + OWN]
            nor[...] = normal[RIM : RIM + OWN]
            inv[...] = jnp.broadcast_to(inverse[RIM : RIM + OWN], inv.shape)

    bands = [slice(n * BAND, (n + 1) * BAND) for n in range(3)]

    def project(weight, result):
        for rows_of in bands:
            result[rows_of] = dot_nt(nx[rows_of], weight[...]).astype(BF16)

    for copy in halo[0]:
        copy.wait_recv()
    arrived(0)
    embed(0)
    slot(zs // 2 + 2)
    embed(1)
    embed(2)
    slot(zs // 2 + 3)
    for n, at in [(5, place_of(0, 3)), (6, place_of(1, 3)), (zs - 1, place_of(0, 4))]:
        arrange(n, at)
    for weight, result in ((wk, kx), (wq, qx), (wv, vx)):
        project(weight, result)
    at_o = half * SPLIT.index("o")

    def out_rows():
        return gb[:, :, :, :, at_o : at_o + half].reshape(width, half)

    for copy in halo[1]:
        copy.wait_recv()
    ext_row = lax.broadcasted_iota(jnp.int32, (BAND, 1), 0) // SIDE - RAD + first_row
    valid = jnp.where(ext_row < lats, 1.0, 0.0).astype(F32)
    for rows_of in bands:
        gx[rows_of] = (dot_nn(cx[rows_of], out_rows()) * valid).astype(BF16)

    scale = 1.0 / math.sqrt(wq.shape[0] // HEADS)
    pairs = HEADS // 2

    low = lax.broadcasted_iota(jnp.int32, (OWN, 128), 1) < 64
    none = jnp.zeros((OWN, 128), BF16)

    def apart(tile):
        return jnp.concatenate([jnp.where(low, tile, none), jnp.where(low, none, tile)], axis=0)

    def together(both):
        return jnp.where(low, both[:OWN], both[OWN:])

    lane = lax.broadcasted_iota(jnp.int32, (OWN, 128), 1)
    known = jnp.zeros((OWN, 128), F32)
    reach = jnp.concatenate([bias[0], bias[0]], axis=0)
    for p in range(pairs):
        tile = slice(p * 128, (p + 1) * 128)
        keys, values = kx[:, tile], vx[:, tile]
        scores = dot_nt(apart(qx[here, tile]), keys) * scale + reach
        top = jnp.max(scores, axis=-1, keepdims=True)
        terms = jnp.exp(scores - top)
        total = jnp.sum(terms, axis=-1, keepdims=True)
        prob = terms / total
        dprob = dot_nt(apart(gx[here, tile]), values)
        delta = jnp.sum(prob * dprob, axis=-1, keepdims=True)
        dscore = (prob * (dprob - delta)).astype(BF16)
        att[:, tile] = together(dot_nn(prob.astype(BF16), values)).astype(BF16)
        dq[:, tile] = together(dot_nn(dscore, keys) * scale).astype(BF16)
        for place, column in ((0, top), (HEADS, total), (2 * HEADS, delta)):
            known = jnp.where(lane == place + 2 * p, column[:OWN], known)
            known = jnp.where(lane == place + 2 * p + 1, column[OWN:], known)

    sx[here] = known
    told = []
    for n, (a, b) in enumerate(around):
        begin, count, place = {1: (OWN - RIM, RIM, 0), -1: (0, RIM, RIM + OWN), 0: (0, OWN, RIM)}[b]
        told.append(send(
            sx.at[pl.ds(HERE + begin, count)], sx.at[pl.ds((1 - a) * BAND + place, count)],
            f_send.at[n], f_recv.at[n], near(a, b),
        ))
    mixed = emb[...] + dot_nt(att[...], out_rows())
    own_row = lax.broadcasted_iota(jnp.int32, (OWN, 1), 0) // SIDE + first_row
    own_valid = jnp.where(own_row < lats, 1.0, 0.0).astype(F32)
    out_ref[...] = (mixed * own_valid).astype(BF16)
    for copy in told:
        copy.wait_recv()

    facts = jnp.transpose(sx[...], (1, 0))
    reach = jnp.concatenate([bias[1], bias[1]], axis=0)
    for p in range(pairs):
        tile = slice(p * 128, (p + 1) * 128)

        def fact(place):
            first = jnp.broadcast_to(facts[place + 2 * p : place + 2 * p + 1, :EXT], (OWN, EXT))
            second = jnp.broadcast_to(facts[place + 2 * p + 1 : place + 2 * p + 2, :EXT], (OWN, EXT))
            return jnp.concatenate([first, second], axis=0)

        queries, grads = qx[:, tile], gx[:, tile]
        scores = dot_nt(apart(kx[here, tile]), queries) * scale + reach
        prob = jnp.exp(scores - fact(0)) / fact(HEADS)
        dprob = dot_nt(apart(vx[here, tile]), grads)
        dscore = (prob * (dprob - fact(2 * HEADS))).astype(BF16)
        dk[:, tile] = together(dot_nn(dscore, queries) * scale).astype(BF16)
        dv[:, tile] = together(dot_nn(prob.astype(BF16), grads)).astype(BF16)

    slope = dot_nn(dq[...], wq[...]) + dot_nn(dk[...], wk[...]) + dot_nn(dv[...], wv[...])
    normal = nor[...]
    centre = jnp.mean(slope, axis=-1, keepdims=True)
    along = jnp.mean(slope * normal, axis=-1, keepdims=True)
    masked = cx[here].astype(F32) * own_valid
    grad_embed = (masked + inv[:, 0:1] * (slope - centre - normal * along)).astype(BF16)
    result = dot_nn(grad_embed, whole[0][...].reshape(width, pads)).astype(BF16)
    grad_ref[...] = result[:, 0:patch_width]

    for copy in sent:
        copy.wait_send()


def body(patches, query_weight, key_weight, value_weight, out_weight, embed_weight, cotangent):
    rows, cols, patch_width = patches.shape
    width = cotangent.shape[-1]
    lons, lats_dev = lax.axis_size("lon"), lax.axis_size("lat")
    zs = lons // 8
    channels = query_weight.shape[1] * lons
    wide_patch = -(-patch_width // 128) * 128
    blocks = (zs, 4, 2, 16)
    vmem = pltpu.VMEM
    dma = pltpu.SemaphoreType.DMA
    out, grad = pl.pallas_call(
        functools.partial(kernel, (lons, lats_dev)),
        out_shape=(
            jax.ShapeDtypeStruct((OWN, width), BF16),
            jax.ShapeDtypeStruct((OWN, patch_width), BF16),
        ),
        in_specs=[pl.BlockSpec(memory_space=pltpu.HBM)] * 7,
        out_specs=(pl.BlockSpec(memory_space=vmem),) * 2,
        scratch_shapes=[
            [vmem(blocks + (wide_patch if name == "e" else width // 2,), BF16) for name in WHOLE],
            vmem(blocks + (len(SPLIT) * (width // 2),), BF16),
            vmem((3, query_weight.shape[1], width), BF16),
            vmem((width // lons, channels), BF16),
            [vmem((OWN, patch_width), BF16), vmem((width // lons, patch_width), BF16)],
            vmem((len(SPLIT), width // lons, channels), BF16),
            vmem((channels, width), BF16),
            vmem((channels, width), BF16),
            vmem((channels, width), BF16),
            vmem((EXT, wide_patch), BF16),
            vmem((EXT, width), BF16),
            vmem((512, 128), F32),
            vmem((EXT, width), BF16),
            vmem((EXT, channels), BF16),
            vmem((EXT, channels), BF16),
            vmem((EXT, channels), BF16),
            vmem((EXT, channels), BF16),
            vmem((OWN, width), F32),
            vmem((OWN, width), F32),
            vmem((OWN, 128), F32),
            vmem((OWN, channels), BF16),
            vmem((OWN, channels), BF16),
            vmem((OWN, channels), BF16),
            vmem((OWN, channels), BF16),
            vmem((2, OWN, EXT), F32),
            dma((len(WHOLE) + 1, 3)),
            dma((len(WHOLE) + 1, 3)),
            dma((len(WHOLE) + 1, 2, zs // 2)),
            dma((len(WHOLE) + 1, 2, zs // 2)),
            dma((zs, 3)),
            dma((zs, 3)),
            dma((len(WHOLE) + 1, zs)),
            dma((len(WHOLE) + 1, zs)),
            dma((2, 4)),
            dma((2, 4)),
            dma((8,)),
            dma((8,)),
            dma((7,)),
        ],
        compiler_params=pltpu.CompilerParams(
            collective_id=0, has_side_effects=True, vmem_limit_bytes=62 * 1024 * 1024
        ),
    )(
        patches.reshape(rows * cols, patch_width),
        query_weight.T,
        key_weight.T,
        value_weight.T,
        out_weight.T,
        embed_weight.T,
        cotangent.reshape(rows * cols, width),
    )
    return out.reshape(rows, cols, width), grad.reshape(rows, cols, patch_width)


def solution(mesh):
    in_specs = (
        P("lat", "lon", None),
        P(None, "lon"),
        P(None, "lon"),
        P(None, "lon"),
        P(None, "lon"),
        P(None, "lon"),
        P("lat", "lon", None),
    )
    out_specs = (P("lat", "lon", None), P("lat", "lon", None))
    return jax.shard_map(body, mesh=mesh, in_specs=in_specs, out_specs=out_specs, check_vma=False)
```

time: 75.8 us -> 66.8 us (0.88)
  the two profiles are of different devices: /device:TPU:1 before, /device:TPU:8 now
where the time goes in v2:
time: 66.8 us; the launch traced here: 66.6 us
  Pallas kernels  63.8 us (96%)
  local copies, waits for them, and re-layouts  2.2 us (3%)
    pallas_call x1, Pallas kernels, body(): pl.pallas_call(functools.partial(kernel, (lons, lats_dev)), out_shape=(ja...  63.8 us
    unnamed x4, local copies, waits for them, and re-layouts  2.2 us

profile of v2, /device:TPU:8, one launch (start us, length us, event | category | flops | bytes accessed | tf_op | source)
XLA Modules:
  0.0 66.6 jit_solution(14881173447525272833)
XLA Ops:
  0.6 63.8 %shard_map.86 = (bf16[64,1024]{1,0:T(8,128)(2,1)}, bf16[64,276]{1,0:T(8,128)(2,1)}) custom-call(bf16[64,276]{1,0:T(8,128)(2,1)} %bitcast.12, bf16[8,1024]{1,0:T(8,128)(2,1)} %bitcast.13, bf16[8,1024]{1,0:T(8,128)(2,1)} %bitcast.14, bf16[8,1024]{1,0:T(8,128)(2,1)} %bitcast.15, bf16[16,512]{1,0:T(8,128)(2,1)} %bitcast.16, bf16[16,276]{1,0:T(8,128)(2,1)} %bitcast.17, ...), custom_call_target="tpu_custom_call" | custom-call | tf_op jit(solution)/shard_map/pallas_call | solution.py:394
  64.4 0.0 copy-start
  64.4 1.6 %copy.11 = bf16[8,8,1024]{2,1,0:T(8,128)(2,1)} copy(bf16[8,8,1024]{2,1,0:T(8,128)(2,1)} %bitcast.10) | data formatting | bytes 262144
  66.0 0.0 copy-done
  66.0 0.6 copy.12
Async XLA Ops:
  64.4 1.6 %copy-start = (bf16[64,276]{1,0:T(8,128)(2,1)S(1)}, bf16[64,276]{1,0:T(8,128)(2,1)}, u32[]{:S(2)}) copy-start(bf16[64,276]{1,0:T(8,128)(2,1)} %get-tuple-element.5) | copy-start | bytes 105988

commit v3 on v2

--- a/solution.py
+++ b/solution.py
@@ -273,11 +273,8 @@
             nor[...] = normal[RIM : RIM + OWN]
             inv[...] = jnp.broadcast_to(inverse[RIM : RIM + OWN], inv.shape)
 
-    bands = [slice(n * BAND, (n + 1) * BAND) for n in range(3)]
-
     def project(weight, result):
-        for rows_of in bands:
-            result[rows_of] = dot_nt(nx[rows_of], weight[...]).astype(BF16)
+        result[...] = dot_nt(nx[...], weight[...]).astype(BF16)
 
     for copy in halo[0]:
         copy.wait_recv()
@@ -300,8 +297,7 @@
         copy.wait_recv()
     ext_row = lax.broadcasted_iota(jnp.int32, (BAND, 1), 0) // SIDE - RAD + first_row
     valid = jnp.where(ext_row < lats, 1.0, 0.0).astype(F32)
-    for rows_of in bands:
-        gx[rows_of] = (dot_nn(cx[rows_of], out_rows()) * valid).astype(BF16)
+    gx[...] = (dot_nn(cx[...], out_rows()) * jnp.concatenate([valid] * 3, axis=0)).astype(BF16)
 
     scale = 1.0 / math.sqrt(wq.shape[0] // HEADS)
     pairs = HEADS // 2
@@ -335,14 +331,11 @@
             known = jnp.where(lane == place + 2 * p, column[:OWN], known)
             known = jnp.where(lane == place + 2 * p + 1, column[OWN:], known)
 
-    sx[here] = known
-    told = []
-    for n, (a, b) in enumerate(around):
-        begin, count, place = {1: (OWN - RIM, RIM, 0), -1: (0, RIM, RIM + OWN), 0: (0, OWN, RIM)}[b]
-        told.append(send(
-            sx.at[pl.ds(HERE + begin, count)], sx.at[pl.ds((1 - a) * BAND + place, count)],
-            f_send.at[n], f_recv.at[n], near(a, b),
-        ))
+    turned = jnp.transpose(jnp.concatenate([known, jnp.zeros((OWN, 128), F32)], axis=0), (1, 0))
+    sx[len(around)] = turned[: 3 * HEADS]
+    told = [
+        send(sx.at[len(around)], sx.at[n], f_send.at[n], f_recv.at[n], near(a, b)) for n, (a, b) in enumerate(around)
+    ]
     mixed = emb[...] + dot_nt(att[...], out_rows())
     own_row = lax.broadcasted_iota(jnp.int32, (OWN, 1), 0) // SIDE + first_row
     own_valid = jnp.where(own_row < lats, 1.0, 0.0).astype(F32)
@@ -350,7 +343,13 @@
     for copy in told:
         copy.wait_recv()
 
-    facts = jnp.transpose(sx[...], (1, 0))
+    strips = []
+    for a in (-1, 0, 1):
+        for b in (-1, 0, 1):
+            n = len(around) if (a, b) == (0, 0) else around.index((-a, -b))
+            begin, end = {-1: (OWN - RIM, OWN), 0: (0, OWN), 1: (0, RIM)}[b]
+            strips.append(sx[n][:, begin:end])
+    facts = jnp.concatenate(strips, axis=1)
     reach = jnp.concatenate([bias[1], bias[1]], axis=0)
     for p in range(pairs):
         tile = slice(p * 128, (p + 1) * 128)
@@ -411,7 +410,7 @@
             vmem((channels, width), BF16),
             vmem((EXT, wide_patch), BF16),
             vmem((EXT, width), BF16),
-            vmem((512, 128), F32),
+            vmem((9, 3 * HEADS, 128), F32),
             vmem((EXT, width), BF16),
             vmem((EXT, channels), BF16),
             vmem((EXT, channels), BF16),

time: 66.8 us -> 63.4 us (0.949)
  Pallas kernels: 63.8 us -> 60.4 us
    pallas_call x1, Pallas kernels: 63.8 us -> 60.4 us  [body(): pl.pallas_call(functools.partial(kernel, (lons, lats_dev)), out_shape=(ja...]
where the time goes in v3:
time: 63.4 us; the launch traced here: 63.3 us
  Pallas kernels  60.4 us (95%)
  local copies, waits for them, and re-layouts  2.2 us (3%)
  between operations  0.65 us (1%)
    pallas_call x1, Pallas kernels, body(): pl.pallas_call(functools.partial(kernel, (lons, lats_dev)), out_shape=(ja...  60.4 us
    unnamed x4, local copies, waits for them, and re-layouts  2.2 us

profile of v3, /device:TPU:8, one launch (start us, length us, event | category | flops | bytes accessed | tf_op | source)
XLA Modules:
  0.0 63.3 jit_solution(3906377551366471740)
XLA Ops:
  0.6 60.4 %shard_map.86 = (bf16[64,1024]{1,0:T(8,128)(2,1)}, bf16[64,276]{1,0:T(8,128)(2,1)}) custom-call(bf16[64,276]{1,0:T(8,128)(2,1)} %bitcast.12, bf16[8,1024]{1,0:T(8,128)(2,1)} %bitcast.13, bf16[8,1024]{1,0:T(8,128)(2,1)} %bitcast.14, bf16[8,1024]{1,0:T(8,128)(2,1)} %bitcast.15, bf16[16,512]{1,0:T(8,128)(2,1)} %bitcast.16, bf16[16,276]{1,0:T(8,128)(2,1)} %bitcast.17, ...), custom_call_target="tpu_custom_call" | custom-call | tf_op jit(solution)/shard_map/pallas_call | solution.py:393
  61.0 0.0 copy-start
  61.0 1.6 %copy.11 = bf16[8,8,1024]{2,1,0:T(8,128)(2,1)} copy(bf16[8,8,1024]{2,1,0:T(8,128)(2,1)} %bitcast.10) | data formatting | bytes 262144
  62.6 0.0 copy-done
  62.6 0.6 copy.12
Async XLA Ops:
  61.0 1.6 %copy-start = (bf16[64,276]{1,0:T(8,128)(2,1)S(1)}, bf16[64,276]{1,0:T(8,128)(2,1)}, u32[]{:S(2)}) copy-start(bf16[64,276]{1,0:T(8,128)(2,1)} %get-tuple-element.5) | copy-start | bytes 105988

commit v4 on v3

--- a/solution.py
+++ b/solution.py
@@ -41,7 +41,7 @@
 
 def kernel(
     sizes, p_ref, q_ref, k_ref, v_ref, o_ref, e_ref, c_ref, out_ref, grad_ref,
-    whole, gb, raw8, raw16, rawp, stage, wk, wq, wv, px, cx, sx, nx, qx, kx, vx, gx, emb, nor, inv, att, dq, dk, dv, bias,
+    whole, gb, raw8, raw16, rawp, stage, wk, wq, wv, px, cx, sx, nx, qx, kx, vx, gx, emb, nor, inv, att, dq, dk, dv, bias, pb, ds, raw, rise,
     y_send, y_recv, z_send, z_recv, x_send, x_recv, s_send, s_recv, h_send, h_recv, f_send, f_recv, l_sem,
 ):
     lons, lats_dev = sizes
@@ -124,7 +124,7 @@
 
     order = ("b", 0)
     last = len(order) - 1
-    soon = 5
+    soon = 7
 
     def lines(part, at):
         return gb.at[at, :, core, :, lanes(0)] if part == "b" else whole[part].at[at, :, core]
@@ -149,22 +149,26 @@
         ]
         if n >= soon:
             ahead[n] = send(source, source, x_send.at[n, 2], x_recv.at[n, 2], at_x(2))
+        go_over("b", n, at)
 
     def go_ahead(n, at):
-        for copy in across[n]:
-            copy.wait_recv()
-        if n >= soon:
-            return
         d = 1 if n % 2 == 0 else -1
-        source = gb.at[at, :, core, :, lanes(-d)]
-        ahead[n] = send(source, source, x_send.at[n, 2], x_recv.at[n, 2], at_x(d))
-
-    def go_over(part, n, at):
-        if part == "b":
-            ahead[n].wait_recv()
-        source = gb.at[at, :, core] if part == "b" else whole[part].at[at, :, core]
+        across[n][0 if d == 1 else 1].wait_recv()
+        if n < soon:
+            source = gb.at[at, :, core, :, lanes(-d)]
+            ahead[n] = send(source, source, x_send.at[n, 2], x_recv.at[n, 2], at_x(d))
+        go_over("b", n, at, -d)
+        across[n][1 if d == 1 else 0].wait_recv()
+        go_over("b", n, at, d)
+
+    def go_last(n, at):
+        ahead[n].wait_recv()
+        go_over("b", n, at, 2)
+
+    def go_over(part, n, at, d=0):
+        source = gb.at[at, :, core, :, lanes(d)] if part == "b" else whole[part].at[at, :, core]
         i = order.index(part)
-        swap[part, n] = send(source, source, s_send.at[i, n], s_recv.at[i, n], sibling)
+        swap[part, n, d] = send(source, source, s_send.at[i, n, d + 1], s_recv.at[i, n, d + 1], sibling)
 
     def came(step, i):
         if step == 1:
@@ -177,7 +181,8 @@
         return [(n if step < zs // 2 + 1 else zs - 1, at) for n, at in came(step, i)]
 
     def arrange(n, at):
-        swap["b", n].wait_recv()
+        for d in (-1, 0, 1, 2):
+            swap["b", n, d].wait_recv()
         for name, weight in (("k", wk), ("q", wq), ("v", wv)):
             begin_lane = half * SPLIT.index(name)
             wide = gb[at, :, :, :, begin_lane : begin_lane + half].astype(F32).reshape(8, 2, 8, half)
@@ -209,19 +214,15 @@
             for n, at in numbers(step - 1, 0):
                 go_ahead(n, at)
                 if n >= soon:
-                    go_over("b", n, at)
+                    go_last(n, at)
         if 1 <= step - 2 <= zs // 2 + 1:
             for n, at in numbers(step - 2, 0):
                 if n < soon:
-                    go_over("b", n, at)
+                    go_last(n, at)
         if 1 <= step - 3 <= zs // 2 + 1:
             for n, at in numbers(step - 3, 0):
-                if n < soon:
+                if n < 5:
                     arrange(n, at)
-
-    def arrived(part):
-        for n in range(zs):
-            swap[part, n].wait_recv()
 
     slot(1)
 
@@ -263,13 +264,13 @@
 
     def embed(n):
         rows_of = slice(n * BAND, (n + 1) * BAND)
-        raw = dot_nt(px[rows_of], whole[0][...].reshape(width, pads))
-        centred = raw - jnp.mean(raw, axis=-1, keepdims=True)
+        patch = dot_nt(px[rows_of], whole[0][...].reshape(width, pads))
+        centred = patch - jnp.mean(patch, axis=-1, keepdims=True)
         inverse = lax.rsqrt(jnp.mean(centred * centred, axis=-1, keepdims=True) + EPS)
         normal = centred * inverse
         nx[rows_of] = normal.astype(BF16)
         if n == 1:
-            emb[...] = raw[RIM : RIM + OWN]
+            emb[...] = patch[RIM : RIM + OWN]
             nor[...] = normal[RIM : RIM + OWN]
             inv[...] = jnp.broadcast_to(inverse[RIM : RIM + OWN], inv.shape)
 
@@ -278,7 +279,8 @@
 
     for copy in halo[0]:
         copy.wait_recv()
-    arrived(0)
+    for n in range(zs):
+        swap[0, n, 0].wait_recv()
     embed(0)
     slot(zs // 2 + 2)
     embed(1)
@@ -324,9 +326,8 @@
         prob = terms / total
         dprob = dot_nt(apart(gx[here, tile]), values)
         delta = jnp.sum(prob * dprob, axis=-1, keepdims=True)
-        dscore = (prob * (dprob - delta)).astype(BF16)
-        att[:, tile] = together(dot_nn(prob.astype(BF16), values)).astype(BF16)
-        dq[:, tile] = together(dot_nn(dscore, keys) * scale).astype(BF16)
+        ds[p] = (prob * (dprob - delta)).astype(BF16)
+        pb[p] = prob.astype(BF16)
         for place, column in ((0, top), (HEADS, total), (2 * HEADS, delta)):
             known = jnp.where(lane == place + 2 * p, column[:OWN], known)
             known = jnp.where(lane == place + 2 * p + 1, column[OWN:], known)
@@ -336,6 +337,14 @@
     told = [
         send(sx.at[len(around)], sx.at[n], f_send.at[n], f_recv.at[n], near(a, b)) for n, (a, b) in enumerate(around)
     ]
+    reach = jnp.concatenate([bias[1], bias[1]], axis=0)
+    for p in range(pairs):
+        tile = slice(p * 128, (p + 1) * 128)
+        att[:, tile] = together(dot_nn(pb[p], vx[:, tile])).astype(BF16)
+        dq[:, tile] = together(dot_nn(ds[p], kx[:, tile]) * scale).astype(BF16)
+        raw[p] = dot_nt(apart(kx[here, tile]), qx[:, tile]) * scale + reach
+        rise[p] = dot_nt(apart(vx[here, tile]), gx[:, tile])
+    slope_q = dot_nn(dq[...], wq[...])
     mixed = emb[...] + dot_nt(att[...], out_rows())
     own_row = lax.broadcasted_iota(jnp.int32, (OWN, 1), 0) // SIDE + first_row
     own_valid = jnp.where(own_row < lats, 1.0, 0.0).astype(F32)
@@ -350,7 +359,6 @@
             begin, end = {-1: (OWN - RIM, OWN), 0: (0, OWN), 1: (0, RIM)}[b]
             strips.append(sx[n][:, begin:end])
     facts = jnp.concatenate(strips, axis=1)
-    reach = jnp.concatenate([bias[1], bias[1]], axis=0)
     for p in range(pairs):
         tile = slice(p * 128, (p + 1) * 128)
 
@@ -360,14 +368,12 @@
             return jnp.concatenate([first, second], axis=0)
 
         queries, grads = qx[:, tile], gx[:, tile]
-        scores = dot_nt(apart(kx[here, tile]), queries) * scale + reach
-        prob = jnp.exp(scores - fact(0)) / fact(HEADS)
-        dprob = dot_nt(apart(vx[here, tile]), grads)
-        dscore = (prob * (dprob - fact(2 * HEADS))).astype(BF16)
+        prob = jnp.exp(raw[p] - fact(0)) / fact(HEADS)
+        dscore = (prob * (rise[p] - fact(2 * HEADS))).astype(BF16)
         dk[:, tile] = together(dot_nn(dscore, queries) * scale).astype(BF16)
         dv[:, tile] = together(dot_nn(prob.astype(BF16), grads)).astype(BF16)
 
-    slope = dot_nn(dq[...], wq[...]) + dot_nn(dk[...], wk[...]) + dot_nn(dv[...], wv[...])
+    slope = slope_q + dot_nn(dk[...], wk[...]) + dot_nn(dv[...], wv[...])
     normal = nor[...]
     centre = jnp.mean(slope, axis=-1, keepdims=True)
     along = jnp.mean(slope * normal, axis=-1, keepdims=True)
@@ -424,14 +430,18 @@
             vmem((OWN, channels), BF16),
             vmem((OWN, channels), BF16),
             vmem((2, OWN, EXT), F32),
+            vmem((HEADS // 2, 2 * OWN, EXT), BF16),
+            vmem((HEADS // 2, 2 * OWN, EXT), BF16),
+            vmem((HEADS // 2, 2 * OWN, EXT), F32),
+            vmem((HEADS // 2, 2 * OWN, EXT), F32),
             dma((len(WHOLE) + 1, 3)),
             dma((len(WHOLE) + 1, 3)),
             dma((len(WHOLE) + 1, 2, zs // 2)),
             dma((len(WHOLE) + 1, 2, zs // 2)),
             dma((zs, 3)),
             dma((zs, 3)),
-            dma((len(WHOLE) + 1, zs)),
-            dma((len(WHOLE) + 1, zs)),
+            dma((len(WHOLE) + 1, zs, 4)),
+            dma((len(WHOLE) + 1, zs, 4)),
             dma((2, 4)),
             dma((2, 4)),
             dma((8,)),

time: 63.4 us -> 61.7 us (0.973)
  Pallas kernels: 60.4 us -> 58.5 us
    pallas_call x1, Pallas kernels: 60.4 us -> 58.5 us  [body(): pl.pallas_call(functools.partial(kernel, (lons, lats_dev)), out_shape=(ja...]
where the time goes in v4:
time: 61.7 us; the launch traced here: 61.4 us
  Pallas kernels  58.5 us (95%)
  local copies, waits for them, and re-layouts  2.2 us (4%)
  between operations  0.65 us (1%)
    pallas_call x1, Pallas kernels, body(): pl.pallas_call(functools.partial(kernel, (lons, lats_dev)), out_shape=(ja...  58.5 us
    unnamed x4, local copies, waits for them, and re-layouts  2.2 us

profile of v4, /device:TPU:8, one launch (start us, length us, event | category | flops | bytes accessed | tf_op | source)
XLA Modules:
  0.0 61.4 jit_solution(16531668207897542443)
XLA Ops:
  0.6 58.5 %shard_map.86 = (bf16[64,1024]{1,0:T(8,128)(2,1)}, bf16[64,276]{1,0:T(8,128)(2,1)}) custom-call(bf16[64,276]{1,0:T(8,128)(2,1)} %bitcast.12, bf16[8,1024]{1,0:T(8,128)(2,1)} %bitcast.13, bf16[8,1024]{1,0:T(8,128)(2,1)} %bitcast.14, bf16[8,1024]{1,0:T(8,128)(2,1)} %bitcast.15, bf16[16,512]{1,0:T(8,128)(2,1)} %bitcast.16, bf16[16,276]{1,0:T(8,128)(2,1)} %bitcast.17, ...), custom_call_target="tpu_custom_call" | custom-call | tf_op jit(solution)/shard_map/pallas_call | solution.py:399
  59.2 0.0 copy-start
  59.2 1.6 %copy.11 = bf16[8,8,1024]{2,1,0:T(8,128)(2,1)} copy(bf16[8,8,1024]{2,1,0:T(8,128)(2,1)} %bitcast.10) | data formatting | bytes 262144
  60.8 0.0 copy-done
  60.8 0.6 %copy.12 = bf16[8,8,276]{2,1,0:T(8,128)(2,1)} copy(bf16[8,8,276]{2,1,0:T(8,128)(2,1)S(1)} %bitcast.11) | data formatting | bytes 70656
Async XLA Ops:
  59.2 1.6 %copy-start = (bf16[64,276]{1,0:T(8,128)(2,1)S(1)}, bf16[64,276]{1,0:T(8,128)(2,1)}, u32[]{:S(2)}) copy-start(bf16[64,276]{1,0:T(8,128)(2,1)} %get-tuple-element.5) | copy-start | bytes 105988

commit v5 on v4

--- a/solution.py
+++ b/solution.py
@@ -256,10 +256,11 @@
     ).astype(F32)
 
     slot(2)
+    slot(3)
     for copy in halo[0] + halo[1]:
         copy.wait_recv()
     halo = sideward(px, 0), sideward(cx, 1)
-    for step in range(3, zs // 2 + 2):
+    for step in range(4, zs // 2 + 2):
         slot(step)
 
     def embed(n):

time: 61.7 us -> 60.4 us (0.979)
  Pallas kernels: 58.5 us -> 57.3 us
    pallas_call x1, Pallas kernels: 58.5 us -> 57.3 us  [body(): pl.pallas_call(functools.partial(kernel, (lons, lats_dev)), out_shape=(ja...]
where the time goes in v5:
time: 60.4 us; the launch traced here: 60.2 us
  Pallas kernels  57.3 us (95%)
  local copies, waits for them, and re-layouts  2.2 us (4%)
  between operations  0.65 us (1%)
    pallas_call x1, Pallas kernels, body(): pl.pallas_call(functools.partial(kernel, (lons, lats_dev)), out_shape=(ja...  57.3 us
    unnamed x4, local copies, waits for them, and re-layouts  2.2 us

profile of v5, /device:TPU:8, one launch (start us, length us, event | category | flops | bytes accessed | tf_op | source)
XLA Modules:
  0.0 60.2 jit_solution(6424085415759639873)
XLA Ops:
  0.6 57.3 %shard_map.86 = (bf16[64,1024]{1,0:T(8,128)(2,1)}, bf16[64,276]{1,0:T(8,128)(2,1)}) custom-call(bf16[64,276]{1,0:T(8,128)(2,1)} %bitcast.12, bf16[8,1024]{1,0:T(8,128)(2,1)} %bitcast.13, bf16[8,1024]{1,0:T(8,128)(2,1)} %bitcast.14, bf16[8,1024]{1,0:T(8,128)(2,1)} %bitcast.15, bf16[16,512]{1,0:T(8,128)(2,1)} %bitcast.16, bf16[16,276]{1,0:T(8,128)(2,1)} %bitcast.17, ...), custom_call_target="tpu_custom_call" | custom-call | tf_op jit(solution)/shard_map/pallas_call | solution.py:400
  58.0 0.0 copy-start
  58.0 1.6 %copy.11 = bf16[8,8,1024]{2,1,0:T(8,128)(2,1)} copy(bf16[8,8,1024]{2,1,0:T(8,128)(2,1)} %bitcast.10) | data formatting | bytes 262144
  59.6 0.0 copy-done
  59.6 0.6 %copy.12 = bf16[8,8,276]{2,1,0:T(8,128)(2,1)} copy(bf16[8,8,276]{2,1,0:T(8,128)(2,1)S(1)} %bitcast.11) | data formatting | bytes 70656
Async XLA Ops:
  58.0 1.6 %copy-start = (bf16[64,276]{1,0:T(8,128)(2,1)S(1)}, bf16[64,276]{1,0:T(8,128)(2,1)}, u32[]{:S(2)}) copy-start(bf16[64,276]{1,0:T(8,128)(2,1)} %get-tuple-element.5) | copy-start | bytes 105988

commit v6 on v5

--- a/solution.py
+++ b/solution.py
@@ -190,8 +190,21 @@
             weight[begin, 0:half] = wide[:, 0].reshape(64, half).astype(BF16)
             weight[begin, half:] = wide[:, 1].reshape(64, half).astype(BF16)
 
+    def hand_on(step):
+        if 1 <= step - 1 <= zs // 2 + 1:
+            for n, at in numbers(step - 1, 0):
+                go_ahead(n, at)
+                if n >= soon:
+                    go_last(n, at)
+        if 1 <= step - 2 <= zs // 2 + 1:
+            for n, at in numbers(step - 2, 0):
+                if n < soon:
+                    go_last(n, at)
+
     def slot(step):
         for i, part in enumerate(order):
+            if i == 1:
+                hand_on(step)
             if step <= zs // 2 + 1:
                 if step == 1:
                     for copy in first[i]:
@@ -210,15 +223,6 @@
                         go_across(n, at)
                     else:
                         go_over(part, n, at)
-        if 1 <= step - 1 <= zs // 2 + 1:
-            for n, at in numbers(step - 1, 0):
-                go_ahead(n, at)
-                if n >= soon:
-                    go_last(n, at)
-        if 1 <= step - 2 <= zs // 2 + 1:
-            for n, at in numbers(step - 2, 0):
-                if n < soon:
-                    go_last(n, at)
         if 1 <= step - 3 <= zs // 2 + 1:
             for n, at in numbers(step - 3, 0):
                 if n < 5:

time: 60.4 us -> 60.4 us (level)
  no operation moved by 1% of the time
where the time goes in v6:
time: 60.4 us; the launch traced here: 60.2 us
  Pallas kernels  57.3 us (95%)
  local copies, waits for them, and re-layouts  2.2 us (4%)
  between operations  0.65 us (1%)
    pallas_call x1, Pallas kernels, body(): pl.pallas_call(functools.partial(kernel, (lons, lats_dev)), out_shape=(ja...  57.3 us
    unnamed x4, local copies, waits for them, and re-layouts  2.2 us

profile of v6, /device:TPU:8, one launch (start us, length us, event | category | flops | bytes accessed | tf_op | source)
XLA Modules:
  0.0 60.2 jit_solution(6985952663131133313)
XLA Ops:
  0.6 57.3 %shard_map.86 = (bf16[64,1024]{1,0:T(8,128)(2,1)}, bf16[64,276]{1,0:T(8,128)(2,1)}) custom-call(bf16[64,276]{1,0:T(8,128)(2,1)} %bitcast.12, bf16[8,1024]{1,0:T(8,128)(2,1)} %bitcast.13, bf16[8,1024]{1,0:T(8,128)(2,1)} %bitcast.14, bf16[8,1024]{1,0:T(8,128)(2,1)} %bitcast.15, bf16[16,512]{1,0:T(8,128)(2,1)} %bitcast.16, bf16[16,276]{1,0:T(8,128)(2,1)} %bitcast.17, ...), custom_call_target="tpu_custom_call" | custom-call | tf_op jit(solution)/shard_map/pallas_call | solution.py:404
  58.0 0.0 copy-start
  58.0 1.6 %copy.11 = bf16[8,8,1024]{2,1,0:T(8,128)(2,1)} copy(bf16[8,8,1024]{2,1,0:T(8,128)(2,1)} %bitcast.10) | data formatting | bytes 262144
  59.6 0.0 copy-done
  59.6 0.6 %copy.12 = bf16[8,8,276]{2,1,0:T(8,128)(2,1)} copy(bf16[8,8,276]{2,1,0:T(8,128)(2,1)S(1)} %bitcast.11) | data formatting | bytes 70656
Async XLA Ops:
  58.0 1.6 %copy-start = (bf16[64,276]{1,0:T(8,128)(2,1)S(1)}, bf16[64,276]{1,0:T(8,128)(2,1)}, u32[]{:S(2)}) copy-start(bf16[64,276]{1,0:T(8,128)(2,1)} %get-tuple-element.5) | copy-start | bytes 105988
